TPU v7x, 512 devices: a whole 4x8x8 slice. The times are simulated.
512 devices in a mesh: req: 64 (over z, y_hi, core), tp: 8 (over y_lo, x).
Axes of the slice: x: 4, y: 8 (y_hi: 4, y_lo: 2; y = y_hi * 2 + y_lo), z: 8, core: 2. Of those that a mesh axis runs over, the one named last changes fastest.
Arguments:
- stale_cache: bfloat16 [64, 128, 2048], P('req', None, 'tp'), may hold values from -6 to 6
- fresh_input: bfloat16 [64, 16, 8192], P('tp', None, 'req'), may hold values from -6 to 6
- kv_weight: bfloat16 [8192, 2048], P('req'), may hold values from -0.0625 to 0.0625
- sel_index: int32 [64, 16], replicated, may hold values from 0 to 127, as said below
- owner: int32 [64], replicated, may hold values from 0 to 63, each once
- retrieval: int32 [512, 4], P('req'), may hold values from 0 to 63
- queries: bfloat16 [512, 32, 8192], P('req', None, 'tp'), may hold values from -90 to 90
- question_kv: bfloat16 [512, 32, 2048], P('req', None, 'tp'), may hold values from -6 to 6
Outputs:
- attended: bfloat16 [512, 32, 8192], P('req', None, 'tp')
Inputs may be any that keep to these rules, and one draw needn't show every extreme that they name: `sel_index`: the positions of one passage are distinct.
All inputs are finite; a program needn't handle non-finite values.
Results may differ from a plain program's by a relative error of at most 0.0056.
Values may be sent and summed in bfloat16 or wider, within the bound.
A program may use at most 64 MiB of HBM per device.

v0:
```python
import math

import jax
import jax.numpy as jnp
from jax import lax
from jax.sharding import PartitionSpec as P

HD = 128


theta_base = 500000.0


def rope(x, pos):
    half = x.shape[-1] // 2
    freqs = theta_base ** (-(jnp.arange(half, dtype=jnp.float32) * 2.0 / x.shape[-1]))
    angle = pos[..., None] * freqs
    cosine = jnp.cos(angle)
    sine = jnp.sin(angle)
    first = x[..., :half]
    second = x[..., half:]
    return jnp.concatenate([first * cosine - second * sine, second * cosine + first * sine], -1)


def blend_all(stale, fresh, sel_rows, head_size):
    count, picked, width = fresh.shape
    heads = width // (2 * head_size)
    parts = fresh.astype(jnp.float32).reshape(count, picked, heads, 2, head_size)
    turned = rope(parts[:, :, :, 0], sel_rows.astype(jnp.float32)[:, :, None])
    fresh_rot = (
        jnp.stack([turned, parts[:, :, :, 1]], 3).reshape(count, picked, width).astype(jnp.bfloat16)
    )
    onehot = sel_rows[:, :, None] == jnp.arange(stale.shape[1], dtype=jnp.int32)[None, None, :]
    placed = jnp.einsum(
        "psl,psc->plc", onehot.astype(jnp.bfloat16), fresh_rot, preferred_element_type=jnp.float32
    )
    hit = jnp.any(onehot, axis=1)[:, :, None]
    return jnp.where(hit, placed.astype(jnp.bfloat16), stale)


def attend_one(query, own_kv, rows_kv, head_size):
    slots, plen, width = rows_kv.shape
    heads = width // (2 * head_size)
    qlen = query.shape[0]
    qheads = query.shape[1] // head_size
    parts = rows_kv.reshape(slots * plen, heads, 2, head_size)
    pos = (jnp.arange(slots * plen, dtype=jnp.int32) // plen * plen).astype(jnp.float32)
    keys = rope(parts[:, :, 0].astype(jnp.float32), pos[:, None]).astype(jnp.bfloat16)
    own = own_kv.reshape(qlen, heads, 2, head_size)
    keys = jnp.concatenate([keys, own[:, :, 0]], 0)
    values = jnp.concatenate([parts[:, :, 1], own[:, :, 1]], 0)
    grouped = query.reshape(qlen, heads, qheads // heads, head_size)
    scores = jnp.einsum(
        "qhgd,khd->hgqk", grouped, keys, preferred_element_type=jnp.float32
    ) / jnp.sqrt(jnp.float32(head_size))
    total = slots * plen + qlen
    kpos = jnp.arange(total, dtype=jnp.int32)
    qpos = jnp.arange(qlen, dtype=jnp.int32)
    allowed = (kpos[None, :] < slots * plen) | (kpos[None, :] - slots * plen <= qpos[:, None])
    scores = jnp.where(allowed, scores, jnp.float32(-1e30))
    top = jnp.max(scores, -1, keepdims=True)
    expo = jnp.exp(scores - top)
    weights = (expo / jnp.sum(expo, -1, keepdims=True)).astype(jnp.bfloat16)
    out = jnp.einsum("hgqk,khd->qhgd", weights, values, preferred_element_type=jnp.float32)
    return out.astype(jnp.bfloat16).reshape(qlen, qheads * head_size)


def local(stale_cache, fresh_input, kv_weight, sel_index, owner, retrieval, queries, question_kv):
    head_size = HD
    partial_kv = jnp.einsum(
        "psd,dc->psc", fresh_input, kv_weight, preferred_element_type=jnp.float32
    )
    summed = lax.psum(partial_kv, "req").astype(jnp.bfloat16)
    fresh_kv = lax.all_to_all(summed, "tp", split_axis=2, concat_axis=0, tiled=True)
    stale_all = lax.all_gather(stale_cache, "req", axis=0, tiled=True)
    blended = blend_all(stale_all, fresh_kv, sel_index, head_size)

    def one_request(query, own_kv, chosen):
        rows = jnp.take(blended, jnp.take(owner, chosen), axis=0)
        return attend_one(query, own_kv, rows, head_size)

    def one_block(items):
        return jax.vmap(one_request)(items[0], items[1], items[2])

    requests = queries.shape[0]
    group = math.gcd(requests, 4)
    blocks = requests // group
    stacked = (
        queries.reshape((blocks, group) + queries.shape[1:]),
        question_kv.reshape((blocks, group) + question_kv.shape[1:]),
        retrieval.reshape((blocks, group) + retrieval.shape[1:]),
    )
    result = lax.map(one_block, stacked)
    return result.reshape((requests,) + result.shape[2:])


def solution(mesh):
    return jax.shard_map(
        local,
        mesh=mesh,
        in_specs=(
            P("req", None, "tp"),
            P("tp", None, "req"),
            P("req", None),
            P(),
            P(),
            P("req", None),
            P("req", None, "tp"),
            P("req", None, "tp"),
        ),
        out_specs=P("req", None, "tp"),
        check_vma=False,
    )
```

profile of v0, /device:TPU:1, one launch (start us, length us, event | category | flops | bytes accessed | tf_op | source)
XLA Modules:
  0.0 373.2 jit_solution(8250323741357081333)
XLA Ops:
  6.5 0.7 all-gather.2.cloned.1.call-update
  7.3 0.3 copy-done
  7.6 1.0 fusion.38
  8.6 294.9 %all-reduce.1 = bf16[8,16,2048]{2,1,0:T(8,128)(2,1)S(1)} all-reduce(f32[8,16,2048]{2,1,0:T(8,128)S(1)} %fusion.38), channel_id=1, replica_groups=mesh['req'=64,'tp'=8] {'req'}, use_global_device_ids=true, to_apply=%region_1.0 | all-reduce | flops 262144 | bytes 1572864 | tf_op jit(solution)/shard_map/psum | solution.py:73
  303.6 4.2 %copy.39 = bf16[8,16,2048]{1,0,2:T(8,128)(2,1)} copy(bf16[8,16,2048]{2,1,0:T(8,128)(2,1)S(1)} %all-reduce.1) | data formatting | bytes 1048576 | tf_op jit(solution)/shard_map/convert_element_type | solution.py:73
  307.7 6.5 %reshape.406 = bf16[8,2,16384]{2,1,0:T(2,128)(2,1)} reshape(bf16[2048,8,16]{2,1,0:T(8,128)(2,1)} %bitcast.134) | data formatting | bytes 1048576
  314.2 4.0 %all-to-all-start = ((bf16[8,2,16384]{2,1,0:T(2,128)(2,1)}), bf16[8,2,16384]{2,1,0:T(2,128)(2,1)S(1)}, u32[]{:S(2)}, u32[]{:S(2)}) async-start(bf16[8,2,16384]{2,1,0:T(2,128)(2,1)} %reshape.406), calls=%async_computation | async-start | bytes 1048576 | tf_op jit(solution)/shard_map/all_to_all | solution.py:74
  318.2 0.1 copy.38
  318.3 0.1 copy.41
  318.4 0.1 copy.46
  318.5 0.2 fusion.40
  318.8 6.6 %all-to-all-done = bf16[8,2,16384]{2,1,0:T(2,128)(2,1)S(1)} async-done(((bf16[8,2,16384]{2,1,0:T(2,128)(2,1)}), bf16[8,2,16384]{2,1,0:T(2,128)(2,1)S(1)}, u32[]{:S(2)}, u32[]{:S(2)}) %all-to-all-start) | async-done | bytes 524320 | tf_op jit(solution)/shard_map/all_to_all | solution.py:74
  325.4 4.1 %reshape.407 = bf16[2048,8,16]{2,1,0:T(8,128)(2,1)} reshape(bf16[8,2,16384]{2,1,0:T(2,128)(2,1)S(1)} %all-to-all-done) | data formatting | bytes 1048576
  329.5 3.9 %copy.40 = bf16[8,16,8,256]{3,1,0,2:T(8,128)(2,1)S(1)} copy(bf16[8,16,8,256]{1,0,3,2:T(8,128)(2,1)} %bitcast.135) | data formatting | bytes 1048576 | tf_op jit(solution)/shard_map/convert_element_type | solution.py:28
  333.4 0.1 convert_element_type.97
  333.5 0.7 slice_convert_fusion
  334.3 2.4 fusion.35
  336.7 0.1 maximum_bitcast_fusion.4
  336.8 0.4 copy.42
  337.2 1.2 pad_maximum_fusion
  338.4 0.3 convert_element_type.99
  338.8 0.0 copy-start.1
  338.8 0.0 all-gather.2.cloned.1.call-done
  338.8 7.1 %convert_select_fusion = bf16[64,128,256]{2,1,0:T(8,128)(2,1)} fusion(bf16[64,128,256]{2,1,0:T(8,128)(2,1)} %all-gather.2.cloned.1.call-done, pred[64,128]{1,0:T(8,128)(4,1)S(1)} %fusion.40, bf16[64,16,256]{2,1,0:T(8,128)(2,1)S(1)} %convert_element_type.99, s32[64,16]{1,0:T(8,128)S(1)} %copy.38), kind=kOutput, calls=%fused_computation.62 | convolution fusion | flops 71434240 | bytes 8925184 | tf_op jit(solution)/shard_map/psl,psc->plc/dot_general | solution.py:34
  346.0 20.3 %while.12 = (s32[]{:T(128)}, bf16[2,4,32,1024]{3,2,1,0:T(8,128)(2,1)}, s32[2,4,4]{2,1,0:T(4,128)S(1)}, s32[64]{0:T(128)S(1)}, bf16[64,128,256]{2,1,0:T(8,128)(2,...) while((s32[]{:T(128)}, bf16[2,4,32,1024]{3,2,1,0:T(8,128)(2,1)}, ...), condition=%wide.region_5.6_spmd, body=%wide.region_2.5_spmd.sunk | while | flops 296723040 | bytes 26791236 | solution.py:93
  346.0 0.1 reshape.421
  346.1 0.7 gather_fusion
  346.8 0.1 gather.28
  346.9 0.1 reshape.422
  346.9 2.8 gather_fusion.1
  349.8 0.3 gather.29
  350.1 0.1 reshape.423
  350.2 0.1 broadcast_bitcast_fusion.2
  350.3 0.5 copy_select_fusion.2
  350.7 0.1 slice_bitcast_fusion.3
  350.9 1.0 multiply_cosine_fusion.3
  351.9 0.4 subtract_convert_fusion.2
  352.4 0.1 fusion.54
  352.6 0.8 fusion.56
  353.5 0.7 fusion.57
  354.2 0.9 fusion.58
  355.1 0.1 copy.71
  355.2 0.1 broadcast_in_dim.108
  355.4 0.0 copy-start.7
  355.4 0.8 copy-done.7
  356.2 0.1 reshape.421
  356.3 0.7 gather_fusion
  356.9 0.1 gather.28
  357.0 0.1 reshape.422
  357.1 2.8 gather_fusion.1
  359.9 0.3 gather.29
  360.2 0.1 reshape.423
  360.3 0.1 broadcast_bitcast_fusion.2
  360.4 0.5 copy_select_fusion.2
  360.9 0.1 slice_bitcast_fusion.3
  361.0 1.0 multiply_cosine_fusion.3
  362.0 0.4 subtract_convert_fusion.2
  362.5 0.1 fusion.54
  362.8 0.8 fusion.56
  363.6 0.7 fusion.57
  364.4 0.9 fusion.58
  365.2 0.1 copy.71
  365.3 0.1 broadcast_in_dim.108
  365.5 0.8 copy-done.7
  (53 shorter events, 0.6 us)
Async XLA Ops:
  6.5 1.0 copy-start
  6.5 332.3 %all-gather.2.cloned.1.call-start = ((), (), s32[]{:S(2)}) async-start(), calls=%async_computation.1 | async-start | bytes 4259840 | tf_op jit(solution)/shard_map/all_gather | solution.py:75
  307.7 10.5 %copy-start.4 = (s32[64,16]{0,1:T(8,128)S(1)}, s32[64,16]{0,1:T(8,128)}, u32[]{:S(2)}) copy-start(s32[64,16]{0,1:T(8,128)} %param.13) | copy-start | bytes 12292
  307.7 10.7 %copy-start.5 = (s32[8,4]{0,1:T(4,128)S(1)}, s32[8,4]{0,1:T(4,128)}, u32[]{:S(2)}) copy-start(s32[8,4]{0,1:T(4,128)} %param.15) | copy-start | bytes 388
  314.2 11.1 %all-to-all-start = ((bf16[8,2,16384]{2,1,0:T(2,128)(2,1)}), bf16[8,2,16384]{2,1,0:T(2,128)(2,1)S(1)}, u32[]{:S(2)}, u32[]{:S(2)}) async-start(bf16[8,2,16384]{2,1,0:T(2,128)(2,1)} %reshape.406), calls=%async_computation | async-start | bytes 1048576 | tf_op jit(solution)/shard_map/all_to_all | solution.py:74
  338.8 7.2 %copy-start.1 = (s32[64]{0:T(128)S(1)}, s32[64]{0:T(128)}, u32[]{:S(2)}) copy-start(s32[64]{0:T(128)} %param.14) | copy-start | bytes 772
  338.8 7.2 %copy-start.2 = (bf16[8,32,1024]{2,1,0:T(8,128)(2,1)S(1)}, bf16[8,32,1024]{2,1,0:T(8,128)(2,1)}, u32[]{:S(2)}) copy-start(bf16[8,32,1024]{2,1,0:T(8,128)(2,1)} %param.16) | copy-start | bytes 1572868
  338.8 7.2 %copy-start.3 = (bf16[8,32,256]{2,1,0:T(8,128)(2,1)S(1)}, bf16[8,32,256]{2,1,0:T(8,128)(2,1)}, u32[]{:S(2)}) copy-start(bf16[8,32,256]{2,1,0:T(8,128)(2,1)} %param.17) | copy-start | bytes 393220
  354.2 1.1 copy-start.6
  355.4 0.8 copy-start.7
  364.4 1.1 copy-start.6
  365.5 0.8 copy-start.7
Sparse Core Ops, SparseCore 0:
  10.7 93.7 all-gather.1
where the time goes:
time: 380 us; the launch traced here: 373 us
  blocking collectives  295 us (78%)
  local copies, waits for them, and re-layouts  31.1 us (8%)
  between operations  13.5 us (4%)
  matrix products  11.6 us (3%)
  other arithmetic  10.4 us (3%)
  waiting for transfers between devices  7.33 us (2%)
  starting transfers between devices  4.01 us (1%)
    psum x1, blocking collectives, local(): summed = lax.psum(partial_kv, 'req').astype(jnp.bfloat16)  295 us
    unnamed x15, local copies, waits for them, and re-layouts  11 us
    gather x10, local copies, waits for them, and re-layouts, one_request(): rows = jnp.take(blended, jnp.take(owner, chosen), axis=0)  7.86 us
  transfers between devices with their start and end apart: 2, of which 1 were waited for; matrix products, arithmetic and copies ran while one was open for 7% of the time, Pallas kernels for 0%

commit v1 on v0

v1 whole, which is shorter than its diff:
```python
import functools
import math

import jax
import jax.numpy as jnp
import numpy as np
from jax import lax
from jax.experimental import pallas as pl
from jax.experimental.pallas import tpu as pltpu
from jax.sharding import PartitionSpec as P

MESH = pl.DeviceIdType.MESH
HD = 128
NZ, NY, NX = 8, 4, 4
PLEN, QLEN, SEL, SLOTS = 128, 32, 16, 4
GROUP = 8
KV = 2 * HD
LAST = SLOTS * PLEN
KEYS = LAST + 128
CHUNK = 64
SCALE = math.log2(math.e) / math.sqrt(HD)
NEG = -1e30
THETA = 500000.0


def trig_tables():
    positions = np.concatenate([np.arange(PLEN), np.arange(8) * PLEN]).astype(np.float32)
    freqs = (THETA ** (-(np.arange(HD // 2, dtype=np.float64) * 2.0 / HD))).astype(np.float32)
    angle = (positions[:, None] * freqs).astype(np.float32).astype(np.float64)
    cosine, sine = np.cos(angle), np.sin(angle)
    return (
        np.concatenate([cosine, cosine], -1).astype(np.float32),
        np.concatenate([-sine, sine], -1).astype(np.float32),
    )


def kernel(
    stale_hbm, x_hbm, w_hbm, sel_hbm, owner_hbm, chosen_hbm, cos_hbm, sin_hbm, q_hbm, own_hbm,
    out_hbm,
    stale_buf, fresh_buf, xbuf, wbuf, zsum, zrecv, bias, trig_c, trig_s,
    kbuf0, vbuf0, kbuf1, vbuf1, sbuf0, pbuf0, sbuf1, pbuf1, tail,
    x_ref, selv_ref, cos_ref, sin_ref, q_ref, own_ref, out_ref, sel_ref, owner_ref, chosen_ref,
    local_sem, out_sem, xy_send, xy_recv, xx_send, xx_recv, w_send, w_recv, wsib,
    sy_send, sy_recv, sz_send, sz_recv, ss_send, ss_recv,
    rz_send, rz_recv, fz_send, fz_recv, fy_send, fy_recv, fs_send, fs_recv,
):
    r, t = lax.axis_index("req"), lax.axis_index("tp")
    z, y, c = r // 8, lax.rem(r, 8) // 2, lax.rem(r, 2)
    ylo, x = t // 4, lax.rem(t, 4)

    def dev(zz, yy, cc, tt):
        return (zz * 8 + yy * 2 + cc, tt)

    def at_z(k):
        return lax.rem(z + k + 2 * NZ, NZ)

    def at_y(k):
        return lax.rem(y + k + 2 * NY, NY)

    sibling = dev(z, y, 1 - c, t)

    def remote(src, dst, send_sem, recv_sem, device):
        return pltpu.make_async_remote_copy(
            src_ref=src, dst_ref=dst, send_sem=send_sem, recv_sem=recv_sem,
            device_id=device, device_id_type=MESH,
        )

    pending = []

    def send(*args):
        copy = remote(*args)
        copy.start()
        pending.append(copy)

    def arrived(dst, recv_sem, send_sem):
        remote(dst, dst, send_sem, recv_sem, sibling).wait_recv()

    plane = [(dy, dl, dc) for dy in range(NY) for dl in range(2) for dc in range(2)][1:]

    def plane_dev(k):
        dy, dl, dc = plane[k]
        yy, ll, cc = at_y(dy), lax.rem(ylo + dl, 2), lax.rem(c + dc, 2)
        return yy, ll, cc

    barrier = pltpu.get_barrier_semaphore()
    peers = []
    for k in range(len(plane)):
        yy, ll, cc = plane_dev(k)
        peers.append(dev(z, yy, cc, ll * 4 + x))
    for k in range(1, NX):
        peers.append((r, ylo * 4 + lax.rem(x + k, NX)))
    for k in range(1, NZ):
        peers.append(dev(at_z(k), y, c, t))
    for peer in peers:
        pl.semaphore_signal(barrier, inc=1, device_id=peer, device_id_type=MESH)

    columns = pl.ds(pl.multiple_of(t * KV, KV), KV)

    def slot(zz, yy):
        return stale_buf.at[zz * 8 + c * 4 + yy]

    def row(zz, cc):
        return stale_buf.at[pl.ds(zz * 8 + cc * 4, 4)]

    def xpiece(ts, ys, cs):
        return xbuf.at[ts, :, pl.ds(pl.multiple_of((cs * 4 + ys) * HD, HD), HD)]

    loads = []
    for source, target in (
        (x_hbm, x_ref), (w_hbm.at[:, columns], wbuf.at[c * 4 + y]), (stale_hbm.at[0], slot(z, y)),
        (sel_hbm, sel_ref), (sel_hbm, selv_ref), (cos_hbm, cos_ref), (sin_hbm, sin_ref),
        (owner_hbm, owner_ref), (chosen_hbm, chosen_ref), (q_hbm, q_ref), (own_hbm, own_ref),
    ):
        loads.append(pltpu.make_async_copy(source, target, local_sem.at[len(loads)]))
        loads[-1].start()
    load_x, load_w, load_stale = loads[:3]
    load_x.wait()
    own_x = pltpu.make_async_copy(x_ref.at[y, c], xpiece(t, y, c), local_sem.at[len(loads)])
    own_x.start()

    pl.semaphore_wait(barrier, len(peers))

    for k in range(len(plane)):
        yy, ll, cc = plane_dev(k)
        send(x_ref.at[yy, cc], xpiece(t, y, c), xy_send.at[k], xy_recv.at[k], dev(z, yy, cc, ll * 4 + x))
    load_w.wait()
    for e in range(1, NY):
        send(wbuf.at[c * 4 + y], wbuf.at[c * 4 + y], w_send.at[e], w_recv.at[e], dev(z, at_y(e), c, t))

    def ring(src, zz, yy, s, d, way):
        step = 1 if way == 0 else -1
        send(src, slot(zz, yy), sz_send.at[way, s, d], sz_recv.at[way, s, d], dev(at_z(step), y, c, t))

    load_stale.wait()
    ring(slot(z, y), z, y, 1, 0, 0)
    ring(slot(z, y), z, y, 1, 0, 1)
    for e in (1, 3, 2):
        send(slot(z, y), slot(z, y), sy_send.at[e], sy_recv.at[e], dev(z, at_y(e), c, t))

    def hop(s, d):
        for way in range(2):
            if s == 4 and (d < 2) != (way == 0):
                continue
            zz, yy = at_z(-s if way == 0 else s), at_y(d)
            arrived(slot(zz, yy), sz_recv.at[way, s, d], sz_send.at[way, s, d])
            if s < 3 or (s == 3 and (d < 2) == (way == 0)):
                ring(slot(zz, yy), zz, yy, s + 1, d, way)

    def share(zz, k):
        send(row(zz, c), row(zz, c), ss_send.at[k], ss_recv.at[k], sibling)

    for load in loads[3:]:
        load.wait()
    place = lax.broadcasted_iota(jnp.int32, (PLEN, 64), 0)
    hit = place == selv_ref[0:1, :]
    for k in range(1, SEL):
        hit = hit | (place == selv_ref[k : k + 1, :])
    bias[...] = jnp.transpose(jnp.where(hit, jnp.float32(NEG), jnp.float32(0.0)))
    for k in range(SEL):
        position = sel_ref[k, r]
        trig_c[pl.ds(k, 1), :] = cos_ref[pl.ds(position, 1), :]
        trig_s[pl.ds(k, 1), :] = sin_ref[pl.ds(position, 1), :]
    col = lax.broadcasted_iota(jnp.int32, (CHUNK, 128), 1)
    token = lax.rem(lax.broadcasted_iota(jnp.int32, (CHUNK, 128), 0), QLEN)
    seen = (col < 64) | ((col < 96) & (col - 64 <= token))
    tail[...] = jnp.where(seen, jnp.float32(0.0), jnp.float32(NEG))
    for buf in (kbuf0, vbuf0, kbuf1, vbuf1):
        buf[LAST + 96 :, :] = jnp.zeros((32, HD), jnp.bfloat16)

    own_x.wait()
    for k in range(len(plane)):
        dy, dl, dc = plane[k]
        ys, ls, cs = at_y(-dy), lax.rem(ylo + dl, 2), lax.rem(c + dc, 2)
        arrived(xpiece(ls * 4 + x, ys, cs), xy_recv.at[k], xy_send.at[k])
    xall = xbuf.reshape(2, 4, SEL, 8 * HD)
    for k in range(1, NX):
        send(xall.at[:, x], xall.at[:, x], xx_send.at[k], xx_recv.at[k], (r, ylo * 4 + lax.rem(x + k, NX)))
    hop(1, 0)
    for e in range(1, NY):
        arrived(wbuf.at[c * 4 + at_y(-e)], w_recv.at[e], w_send.at[e])
    mine_w = wbuf.at[pl.ds(c * 4, 4)]
    send(mine_w, mine_w, wsib.at[0], wsib.at[1], sibling)
    for e in (3, 1, 2):
        d = (NY - e) % NY
        arrived(slot(z, at_y(d)), sy_recv.at[e], sy_send.at[e])
        ring(slot(z, at_y(d)), z, at_y(d), 1, d, 0)
        ring(slot(z, at_y(d)), z, at_y(d), 1, d, 1)
    share(z, 0)
    hop(2, 0)
    for k in range(1, NX):
        xs = lax.rem(x + NX - k, NX)
        arrived(xall.at[:, xs], xx_recv.at[k], xx_send.at[k])
    arrived(wbuf.at[pl.ds((1 - c) * 4, 4)], wsib.at[1], wsib.at[0])
    part = jnp.dot(
        xbuf[...].reshape(NZ * SEL, 8 * HD),
        wbuf[...].reshape(8 * HD, KV),
        preferred_element_type=jnp.float32,
    )
    zsum[...] = part.reshape(NZ, SEL, KV)
    for k in range(1, NZ):
        send(zsum.at[at_z(k)], zrecv.at[k], rz_send.at[k], rz_recv.at[k], dev(at_z(k), y, c, t))
    for d in (1, 3, 2):
        hop(1, d)
    share(at_z(-1), 1)
    share(at_z(1), 2)

    total = zsum[z]
    for k in range(1, NZ):
        arrived(zrecv.at[k], rz_recv.at[k], rz_send.at[k])
        total = total + zrecv[k]
    fresh = total.astype(jnp.bfloat16).astype(jnp.float32)
    keys = fresh[:, :HD]
    keys = keys * trig_c[...] + pltpu.roll(keys, HD // 2, 1) * trig_s[...]

    def fslot(yy, zz):
        return fresh_buf.at[c * 4 + yy, zz]

    fresh_buf[c * 4 + y, z, :, :HD] = keys.astype(jnp.bfloat16)
    fresh_buf[c * 4 + y, z, :, HD:] = fresh[:, HD:].astype(jnp.bfloat16)
    for k in range(1, NZ):
        send(fslot(y, z), fslot(y, z), fz_send.at[k], fz_recv.at[k], dev(at_z(k), y, c, t))

    hop(3, 0)
    for d in (1, 3, 2):
        hop(2, d)
    share(at_z(-2), 3)
    share(at_z(2), 4)

    for k in range(1, NZ):
        arrived(fslot(y, at_z(-k)), fz_recv.at[k], fz_send.at[k])

    def fcol(yy, cc):
        return fresh_buf.at[cc * 4 + yy]

    for e in (1, 3, 2):
        send(fcol(y, c), fcol(y, c), fy_send.at[e], fy_recv.at[e], dev(z, at_y(e), c, t))
    send(fcol(y, c), fcol(y, c), fs_send.at[0], fs_recv.at[0], sibling)

    for d in (1, 3, 2):
        hop(3, d)
    share(at_z(-3), 5)
    share(at_z(3), 6)
    for e in (3, 1, 2):
        yy = at_y(-e)
        arrived(fcol(yy, c), fy_recv.at[e], fy_send.at[e])
        send(fcol(yy, c), fcol(yy, c), fs_send.at[e], fs_recv.at[e], sibling)
    for d in (0, 1, 3, 2):
        hop(4, d)
    share(at_z(4), 7)

    for e in range(NY):
        arrived(fcol(at_y(-e), 1 - c), fs_recv.at[e], fs_send.at[e])
    for k, far in enumerate((0, -1, 1, -2, 2, -3, 3, 4)):
        arrived(row(at_z(far), 1 - c), ss_recv.at[k], ss_send.at[k])
    for copy in pending:
        copy.wait_send()

    def turn(block, j):
        wide = block.astype(jnp.float32)
        wide = wide * cos_ref[pl.ds(PLEN + j, 1), :] + pltpu.roll(wide, HD // 2, 1) * sin_ref[pl.ds(PLEN + j, 1), :]
        return wide.astype(jnp.bfloat16)

    def assemble(i, kbuf, vbuf):
        biases = []
        for j in range(SLOTS):
            o = owner_ref[chosen_ref[j, i]]
            oz, oy, oc = o // 8, lax.rem(o, 8) // 2, lax.rem(o, 2)
            old = stale_buf[oz * 8 + oc * 4 + oy]
            new = fresh_buf[oc * 4 + oy, oz]
            biases.append(bias[pl.ds(o, 1), :])
            old_key, new_key = old[:, :HD], new[:, :HD]
            if j:
                old_key, new_key = turn(old_key, j), turn(new_key, j)
            kbuf[j * PLEN : (j + 1) * PLEN, :] = old_key
            vbuf[j * PLEN : (j + 1) * PLEN, :] = old[:, HD:]
            kbuf[LAST + j * SEL : LAST + (j + 1) * SEL, :] = new_key
            vbuf[LAST + j * SEL : LAST + (j + 1) * SEL, :] = new[:, HD:]
        own = own_ref[i]
        kbuf[LAST + 64 : LAST + 96, :] = own[:, :HD]
        vbuf[LAST + 64 : LAST + 96, :] = own[:, HD:]
        return jnp.concatenate(biases, 1)

    def score(i, kbuf, sbuf):
        query = q_ref[i]
        query = jnp.concatenate([query[:, h * HD : (h + 1) * HD] for h in range(GROUP)], 0)
        sbuf[...] = lax.dot_general(
            query, kbuf[...], (((1,), (1,)), ((), ())), preferred_element_type=jnp.float32
        )

    def soften(masked, sbuf, pbuf):
        for first in range(0, GROUP * QLEN, CHUNK):
            part_rows = slice(first, first + CHUNK)
            raw = jnp.concatenate([sbuf[part_rows, :LAST] + masked, sbuf[part_rows, LAST:] + tail[...]], 1)
            expo = jnp.exp2((raw - jnp.max(raw, 1, keepdims=True)) * SCALE)
            pbuf[part_rows, :] = (expo * (1.0 / jnp.sum(expo, 1, keepdims=True))).astype(jnp.bfloat16)

    def weigh(i, vbuf, pbuf):
        result = jnp.dot(pbuf[...], vbuf[...], preferred_element_type=jnp.float32).astype(jnp.bfloat16)
        for h in range(GROUP):
            out_ref[i, :, h * HD : (h + 1) * HD] = result[h * QLEN : (h + 1) * QLEN]

    def store(i):
        return pltpu.make_async_copy(out_ref.at[i], out_hbm.at[i], out_sem.at[i])

    def pair(p, carry):
        i0, i1 = 2 * p, 2 * p + 1
        masked0 = assemble(i0, kbuf0, vbuf0)
        masked1 = assemble(i1, kbuf1, vbuf1)
        score(i0, kbuf0, sbuf0)
        score(i1, kbuf1, sbuf1)
        soften(masked0, sbuf0, pbuf0)
        weigh(i0, vbuf0, pbuf0)
        soften(masked1, sbuf1, pbuf1)
        weigh(i1, vbuf1, pbuf1)
        store(i0).start()
        store(i1).start()
        return carry

    lax.fori_loop(0, 4, pair, 0)
    for i in range(8):
        store(i).wait()


def local(stale, fresh_input, kv_weight, sel_index, owner, retrieval, queries, question_kv):
    cosine, sine = trig_tables()
    any_spec = pl.BlockSpec(memory_space=pl.ANY)
    dma = pltpu.SemaphoreType.DMA
    return pl.pallas_call(
        kernel,
        out_shape=jax.ShapeDtypeStruct(queries.shape, jnp.bfloat16),
        in_specs=[any_spec] * 10,
        out_specs=any_spec,
        scratch_shapes=[
            pltpu.VMEM((64, PLEN, KV), jnp.bfloat16),
            pltpu.VMEM((8, NZ, SEL, KV), jnp.bfloat16),
            pltpu.VMEM((8, SEL, 8 * HD), jnp.bfloat16),
            pltpu.VMEM((8, HD, KV), jnp.bfloat16),
            pltpu.VMEM((NZ, SEL, KV), jnp.float32),
            pltpu.VMEM((NZ, SEL, KV), jnp.float32),
            pltpu.VMEM((64, PLEN), jnp.float32),
            pltpu.VMEM((SEL, HD), jnp.float32),
            pltpu.VMEM((SEL, HD), jnp.float32),
            pltpu.VMEM((KEYS, HD), jnp.bfloat16),
            pltpu.VMEM((KEYS, HD), jnp.bfloat16),
            pltpu.VMEM((KEYS, HD), jnp.bfloat16),
            pltpu.VMEM((KEYS, HD), jnp.bfloat16),
            pltpu.VMEM((GROUP * QLEN, KEYS), jnp.float32),
            pltpu.VMEM((GROUP * QLEN, KEYS), jnp.bfloat16),
            pltpu.VMEM((GROUP * QLEN, KEYS), jnp.float32),
            pltpu.VMEM((GROUP * QLEN, KEYS), jnp.bfloat16),
            pltpu.VMEM((CHUNK, 128), jnp.float32),
            pltpu.VMEM((NY, 2, SEL, HD), jnp.bfloat16),
            pltpu.VMEM((SEL, 64), jnp.int32),
            pltpu.VMEM(cosine.shape, jnp.float32),
            pltpu.VMEM(sine.shape, jnp.float32),
            pltpu.VMEM(queries.shape, jnp.bfloat16),
            pltpu.VMEM(question_kv.shape, jnp.bfloat16),
            pltpu.VMEM(queries.shape, jnp.bfloat16),
            pltpu.SMEM((SEL, 64), jnp.int32),
            pltpu.SMEM((64,), jnp.int32),
            pltpu.SMEM((SLOTS, 8), jnp.int32),
            dma((12,)),
            dma((8,)),
            dma((15,)), dma((15,)),
            dma((NX,)), dma((NX,)),
            dma((NY,)), dma((NY,)),
            dma((2,)),
            dma((NY,)), dma((NY,)),
            dma((2, 5, NY)), dma((2, 5, NY)),
            dma((8,)), dma((8,)),
            dma((NZ,)), dma((NZ,)),
            dma((NZ,)), dma((NZ,)),
            dma((NY,)), dma((NY,)),
            dma((NY,)), dma((NY,)),
        ],
        compiler_params=pltpu.CompilerParams(
            collective_id=0, has_side_effects=True, vmem_limit_bytes=62 * 1024 * 1024
        ),
    )(
        stale,
        fresh_input.reshape(NY, 2, SEL, HD),
        kv_weight,
        sel_index.T,
        owner,
        retrieval.T,
        jnp.asarray(cosine),
        jnp.asarray(sine),
        queries,
        question_kv,
    )


def solution(mesh):
    return jax.shard_map(
        local,
        mesh=mesh,
        in_specs=(
            P("req", None, "tp"),
            P("tp", None, "req"),
            P("req", None),
            P(),
            P(),
            P("req", None),
            P("req", None, "tp"),
            P("req", None, "tp"),
        ),
        out_specs=P("req", None, "tp"),
        check_vma=False,
    )
```

time: 380 us -> 63.5 us (0.17); the launches traced: 373 us -> 63.3 us
  blocking collectives: 295 us -> 0 us
  Pallas kernels: 0 us -> 61.4 us
  local copies, waits for them, and re-layouts: 31.1 us -> 1.87 us
  between operations: 13.5 us -> 0.01 us
  matrix products: 11.6 us -> 0 us
  other arithmetic: 10.4 us -> 0 us
  waiting for transfers between devices: 7.33 us -> 0 us
  starting transfers between devices: 4.01 us -> 0 us
    psum x1 -> x0, blocking collectives: 295 us -> none  [local(): summed = lax.psum(partial_kv, 'req').astype(jnp.bfloat16)]
    pallas_call x0 -> x1, Pallas kernels: none -> 61.4 us  [local(): pl.pallas_call(kernel, out_shape=jax.ShapeDtypeStruct(queries.shape, jnp....]
    dot_general x6 -> x0, matrix products: 11.6 us -> none  [the longest x1 7.13 us: blend_all(): jnp.einsum('psl,psc->plc', onehot.astype(jnp.bfloat16), fresh_rot, prefer...]
    unnamed x15 -> x1, local copies, waits for them, and re-layouts: 11 us -> 1.87 us
    convert_element_type x7 -> x0, local copies, waits for them, and re-layouts: 8.88 us -> none  [the longest x1 4.18 us: local(): summed = lax.psum(partial_kv, 'req').astype(jnp.bfloat16)]
    gather x10 -> x0, local copies, waits for them, and re-layouts: 7.86 us -> none  [one_request(): rows = jnp.take(blended, jnp.take(owner, chosen), axis=0)]
    all_to_all x1 -> x0, waiting for transfers between devices: 6.6 us -> none  [local(): lax.all_to_all(summed, 'tp', split_axis=2, concat_axis=0, tiled=True)]
    another operation x5 -> x0, other arithmetic: 4.58 us -> none
  transfers between devices with their start and end apart: 2 -> 0, of which waited for: 1 -> 0; matrix products, arithmetic and copies ran while one was open for 7% -> 0% of each run, Pallas kernels for 0% -> 0%
where the time goes in v1:
time: 63.5 us; the launch traced here: 63.3 us
  Pallas kernels  61.4 us (97%)
  local copies, waits for them, and re-layouts  1.87 us (3%)
    pallas_call x1, Pallas kernels, local(): pl.pallas_call(kernel, out_shape=jax.ShapeDtypeStruct(queries.shape, jnp....  61.4 us
    unnamed x1, local copies, waits for them, and re-layouts  1.87 us

profile of v1, /device:TPU:1, one launch (start us, length us, event | category | flops | bytes accessed | tf_op | source)
XLA Modules:
  0.0 63.3 jit_solution(11743171688999950799)
XLA Ops:
  0.0 61.4 %shard_map.100 = bf16[8,32,1024]{2,1,0:T(8,128)(2,1)} custom-call(bf16[1,128,256]{2,1,0:T(8,128)(2,1)} %stale_hbm.1, bf16[4,2,16,128]{3,2,1,0:T(8,128)(2,1)} %bitcast.3, bf16[128,2048]{1,0:T(8,128)(2,1)} %w_hbm.1, s32[16,64]{1,0:T(8,128)} %bitcast.4, s32[64]{0:T(128)} %owner_hbm.1, s32[4,8]{1,0:T(4,128)} %bitcast.5, f32[136,128]{1,0:T(8,128)} %constant.4.clone.cos_hbm, ...), custom_call_target="tpu_custom_call" | custom-call | tf_op jit(solution)/shard_map/pallas_call | solution.py:328
  61.4 1.9 %copy.12 = bf16[8,32,1024]{2,1,0:T(8,128)(2,1)} copy(bf16[8,32,1024]{2,1,0:T(8,128)(2,1)} %shard_map.100) | data formatting | bytes 1048576

commit v2 on v0

v2 whole, which is shorter than its diff:
```python
import functools
import math

import jax
import jax.numpy as jnp
import numpy as np
from jax import lax
from jax.experimental import pallas as pl
from jax.experimental.pallas import tpu as pltpu
from jax.sharding import PartitionSpec as P

MESH = pl.DeviceIdType.MESH
HD = 128
NZ, NY, NX = 8, 4, 4
PLEN, QLEN, SEL, SLOTS = 128, 32, 16, 4
GROUP = 8
KV = 2 * HD
LAST = SLOTS * PLEN
KEYS = LAST + 128
KEPT = PLEN - SEL
CHUNK = 64
SCALE = math.log2(math.e) / math.sqrt(HD)
NEG = -1e30
THETA = 500000.0


def trig_tables():
    positions = np.concatenate([np.arange(PLEN), np.arange(8) * PLEN]).astype(np.float32)
    freqs = (THETA ** (-(np.arange(HD // 2, dtype=np.float64) * 2.0 / HD))).astype(np.float32)
    angle = (positions[:, None] * freqs).astype(np.float32).astype(np.float64)
    cosine, sine = np.cos(angle), np.sin(angle)
    return (
        np.concatenate([cosine, cosine], -1).astype(np.float32),
        np.concatenate([-sine, sine], -1).astype(np.float32),
    )


def gather_kernel(
    stale_hbm, x_hbm, w_hbm, sel_hbm, cos_hbm, sin_hbm,
    pas,
    stale_ref, own_rows, own_fresh, xbuf, wbuf, zsum, zrecv, trig_c, trig_s, x_ref, w_ref, cos_ref, sin_ref, sel_ref,
    local_sem, xy_send, xy_recv, xx_send, xx_recv, w_send, w_recv, wr_send, wr_recv,
    seed_send, seed_recv, yr_send, yr_recv, sz_send, sz_recv, ss_send, ss_recv,
    rz_send, rz_recv, fz_send, fz_recv, fy_send, fy_recv, fr_send, fr_recv, fs_send, fs_recv,
):
    r, t = lax.axis_index("req"), lax.axis_index("tp")
    z, y, c = r // 8, lax.rem(r, 8) // 2, lax.rem(r, 2)
    ylo, x = t // 4, lax.rem(t, 4)

    def dev(zz, yy, cc, tt):
        return (zz * 8 + yy * 2 + cc, tt)

    def at_z(k):
        return lax.rem(z + k + 2 * NZ, NZ)

    def at_y(k):
        return lax.rem(y + k + 2 * NY, NY)

    def at_x(k):
        return lax.rem(x + k + 2 * NX, NX)

    def other(dl):
        return lax.rem(ylo + dl, 2)

    def remote(src, dst, send_sem, recv_sem, device):
        return pltpu.make_async_remote_copy(
            src_ref=src, dst_ref=dst, send_sem=send_sem, recv_sem=recv_sem,
            device_id=device, device_id_type=MESH,
        )

    def arrived(dst, recv_sem, send_sem):
        remote(dst, dst, send_sem, recv_sem, dev(z, y, 1 - c, t)).wait_recv()

    def send(pending, *args):
        copy = remote(*args)
        copy.start()
        pending.append(copy)

    line = [(dy, dl) for dy in range(NY) for dl in range(2)]
    sides = [(0, 1), (0, -1), (1, 0), (-1, 0)]

    barrier = pltpu.get_barrier_semaphore()

    def greet(device):
        pl.semaphore_signal(barrier, inc=1, device_id=device, device_id_type=MESH)

    @pl.when(c == 0)
    def _():
        for dz, dy in sides:
            for cc in range(2):
                greet(dev(at_z(dz), at_y(dy), cc, t))
        greet(dev(z, y, 1, t))

    @pl.when(c == 1)
    def _():
        for dy, dl in line[1:]:
            for cc in range(2):
                greet(dev(z, at_y(dy), cc, other(dl) * 4 + x))
        greet(dev(z, y, 0, t))
        for k in range(1, NX):
            greet((r, ylo * 4 + at_x(k)))
        for k in range(1, NZ):
            greet(dev(at_z(k), y, 1, t))

    columns = pl.ds(pl.multiple_of(t * KV, KV), KV)

    def chunk(zz, yy):
        return pas.at[zz, yy, :, pl.ds(0, KEPT)]

    def kept(zz, yy, cc):
        return pas.at[zz, yy, cc, pl.ds(0, KEPT)]

    def column(yy):
        return pas.at[:, yy, :, pl.ds(KEPT, SEL)]

    def half_column(yy, cc):
        return pas.at[:, yy, cc, pl.ds(KEPT, SEL)]

    def fresh_slot(zz):
        return pas.at[zz, y, :, pl.ds(KEPT, SEL)]

    def xpiece(ts, ys, cs):
        return xbuf.at[ts, :, :, pl.ds(pl.multiple_of((ys * 2 + cs) * HD, HD), HD)]

    def wpiece(ys, cs):
        return wbuf.at[ys, cs]

    loads = []

    def load(source, target):
        copy = pltpu.make_async_copy(source, target, local_sem.at[len(loads)])
        copy.start()
        loads.append(copy)
        return copy

    load_sel = load(sel_hbm, sel_ref)
    load_stale = load(stale_hbm.at[0], stale_ref)
    load_x = load(x_hbm, x_ref)
    load_w = load(w_hbm.at[:, columns], w_ref)
    load_cos = load(cos_hbm, cos_ref)
    load_sin = load(sin_hbm, sin_ref)

    load_sel.wait()
    lane = lax.broadcasted_iota(jnp.int32, (8, PLEN), 1)
    hit = lane == sel_ref[0, r]
    for k in range(1, SEL):
        hit = hit | (lane == sel_ref[k, r])
    keep = jnp.where(hit, jnp.float32(0.0), jnp.float32(1.0))
    before = lax.broadcasted_iota(jnp.int32, (PLEN, PLEN), 0) < lax.broadcasted_iota(jnp.int32, (PLEN, PLEN), 1)
    rank = jnp.dot(
        keep.astype(jnp.bfloat16),
        jnp.where(before, jnp.float32(1.0), jnp.float32(0.0)).astype(jnp.bfloat16),
        preferred_element_type=jnp.float32,
    )
    order = lax.broadcasted_iota(jnp.int32, (KEPT, PLEN), 0).astype(jnp.float32)
    picked = jnp.where(order == rank[0:1], keep[0:1], jnp.float32(0.0)).astype(jnp.bfloat16)
    load_stale.wait()
    own_rows[...] = jnp.dot(picked, stale_ref[...], preferred_element_type=jnp.float32).astype(jnp.bfloat16)
    load_x.wait()
    load_w.wait()
    load_cos.wait()
    load_sin.wait()

    @pl.when(c == 0)
    def _():
        pl.semaphore_wait(barrier, 12)

    @pl.when(c == 1)
    def _():
        pl.semaphore_wait(barrier, 22)

    started = []
    for k, (dy, dl) in enumerate(line[1:]):
        send(
            started, x_ref.at[at_y(dy)], xpiece(t, y, c), xy_send.at[k + 1], xy_recv.at[k + 1, c],
            dev(z, at_y(dy), 1, other(dl) * 4 + x),
        )
    for k in (2, 3, 0, 1):
        dz, dy = sides[k]
        send(
            started, own_rows, kept(z, y, c), seed_send.at[k], seed_recv.at[k, c], dev(at_z(dz), at_y(dy), 0, t)
        )
    for k in range(2):
        send(
            started, w_ref, wpiece(y, c), w_send.at[k], w_recv.at[k, c], dev(z, at_y(sides[k][1]), 1, t)
        )

    @pl.when(c == 0)
    def _():
        pending = []
        mate = dev(z, y, 1, t)
        send(pending, x_ref.at[y], xpiece(t, y, 0), xy_send.at[0], xy_recv.at[0, 0], mate)
        send(pending, w_ref, wpiece(y, 0), w_send.at[2], w_recv.at[2, 0], mate)
        own_copy = pltpu.make_async_copy(own_rows, kept(z, y, 0), local_sem.at[len(loads)])
        own_copy.start()

        def ring(zz, yy, s, d, way):
            step = 1 if way == 0 else -1
            send(
                pending, chunk(zz, yy), chunk(zz, yy), sz_send.at[way, s, d], sz_recv.at[way, s, d],
                dev(at_z(step), y, 0, t),
            )

        def share(zz, yy, rel, d):
            send(pending, chunk(zz, yy), chunk(zz, yy), ss_send.at[rel, d], ss_recv.at[rel, d], mate)

        def inject(d):
            for way in range(2):
                ring(z, at_y(d), 1, d, way)
            share(z, at_y(d), 0, d)

        def hop(s, d):
            for way in range(2):
                if s == 4 and (d < 2) != (way == 0):
                    continue
                rel = (-s if way == 0 else s) % NZ
                zz, yy = at_z(rel), at_y(d)
                if s == 1 and d == 0:
                    for cc in range(2):
                        arrived(kept(zz, yy, cc), seed_recv.at[2 + way, cc], seed_send.at[2 + way])
                else:
                    arrived(chunk(zz, yy), sz_recv.at[way, s, d], sz_send.at[way, s, d])
                if s < 3 or (s == 3 and (d < 2) == (way == 0)):
                    ring(zz, yy, s + 1, d, way)
                share(zz, yy, rel, d)

        hop(1, 0)
        for k in range(2):
            yy = at_y(-sides[k][1])
            for cc in range(2):
                arrived(kept(z, yy, cc), seed_recv.at[k, cc], seed_send.at[k])
            send(
                pending, kept(z, yy, k), kept(z, yy, k), yr_send.at[k], yr_recv.at[k],
                dev(z, at_y(sides[k][1]), 0, t),
            )
            inject(3 if k == 0 else 1)
        hop(2, 0)
        hop(1, 3)
        hop(1, 1)
        for k in range(2):
            arrived(kept(z, at_y(2), k), yr_recv.at[k], yr_send.at[k])
        inject(2)
        own_copy.wait()
        arrived(kept(z, y, 1), ss_recv.at[0, 0], ss_send.at[0, 0])
        send(pending, kept(z, y, 0), kept(z, y, 0), ss_send.at[0, 0], ss_recv.at[0, 0], mate)
        for s, d in (
            (3, 0), (2, 3), (2, 1), (1, 2), (4, 0), (3, 3), (3, 1), (2, 2), (4, 3), (4, 1), (3, 2), (4, 2),
        ):
            hop(s, d)
        for d in range(NY):
            arrived(column(at_y(d)), fs_recv.at[d], fs_send.at[d])
        for copy in pending:
            copy.wait_send()

    @pl.when(c == 1)
    def _():
        pending = []
        mate = dev(z, y, 0, t)
        own_x = pltpu.make_async_copy(x_ref.at[y], xpiece(t, y, 1), local_sem.at[len(loads)])
        own_w = pltpu.make_async_copy(w_ref, wpiece(y, 1), local_sem.at[len(loads) + 1])
        own_copy = pltpu.make_async_copy(own_rows, kept(z, y, 1), local_sem.at[len(loads) + 2])
        own_x.start()
        own_w.start()
        own_copy.start()
        send(pending, own_rows, kept(z, y, 1), ss_send.at[0, 0], ss_recv.at[0, 0], mate)
        own_x.wait()
        arrived(xpiece(t, y, 0), xy_recv.at[0, 0], xy_send.at[0])
        for k, (dy, dl) in enumerate(line[1:]):
            for cc in range(2):
                arrived(xpiece(other(dl) * 4 + x, at_y(-dy), cc), xy_recv.at[k + 1, cc], xy_send.at[k + 1])
        xall = xbuf.reshape(2, 4, 2, SEL, 8 * HD)
        for k in range(1, NX):
            send(
                pending, xall.at[:, x], xall.at[:, x], xx_send.at[k], xx_recv.at[k], (r, ylo * 4 + at_x(k))
            )
        for k in range(2):
            yy = at_y(-sides[k][1])
            for cc in range(2):
                arrived(wpiece(yy, cc), w_recv.at[k, cc], w_send.at[k])
            send(
                pending, wpiece(yy, k), wpiece(yy, k), wr_send.at[k], wr_recv.at[k],
                dev(z, at_y(sides[k][1]), 1, t),
            )
        for cc in range(2):
            for k in range(SEL):
                position = sel_ref[k, r - 1 + cc]
                trig_c[cc, pl.ds(k, 1), :] = cos_ref[pl.ds(position, 1), :]
                trig_s[cc, pl.ds(k, 1), :] = sin_ref[pl.ds(position, 1), :]
        own_w.wait()
        arrived(wpiece(y, 0), w_recv.at[2, 0], w_send.at[2])
        for k in range(1, NX):
            arrived(xall.at[:, at_x(-k)], xx_recv.at[k], xx_send.at[k])
        for k in range(2):
            arrived(wpiece(at_y(2), k), wr_recv.at[k], wr_send.at[k])
        part = jnp.dot(
            xbuf[...].reshape(NZ * 2 * SEL, 8 * HD),
            wbuf[...].reshape(8 * HD, KV),
            preferred_element_type=jnp.float32,
        )
        zsum[...] = part.reshape(NZ, 2, SEL, KV)
        for k in range(1, NZ):
            send(
                pending, zsum.at[at_z(k)], zrecv.at[k], rz_send.at[k], rz_recv.at[k], dev(at_z(k), y, 1, t)
            )
        total = zsum[z]
        for k in range(1, NZ):
            arrived(zrecv.at[k], rz_recv.at[k], rz_send.at[k])
            total = total + zrecv[k]
        fresh = total.astype(jnp.bfloat16).astype(jnp.float32)
        for cc in range(2):
            keys = fresh[cc, :, :HD]
            keys = keys * trig_c[cc] + pltpu.roll(keys, HD // 2, 1) * trig_s[cc]
            own_fresh[cc, :, :HD] = keys.astype(jnp.bfloat16)
            own_fresh[cc, :, HD:] = fresh[cc, :, HD:].astype(jnp.bfloat16)
        for k in range(1, NZ):
            send(pending, own_fresh, fresh_slot(z), fz_send.at[k], fz_recv.at[k], dev(at_z(k), y, 1, t))
        keep_fresh = pltpu.make_async_copy(own_fresh, fresh_slot(z), local_sem.at[len(loads) + 3])
        keep_fresh.start()
        keep_fresh.wait()
        for k in range(1, NZ):
            arrived(fresh_slot(at_z(-k)), fz_recv.at[k], fz_send.at[k])

        def share(d):
            send(pending, column(at_y(d)), column(at_y(d)), fs_send.at[d], fs_recv.at[d], mate)

        for k in range(2):
            send(
                pending, column(y), column(y), fy_send.at[k], fy_recv.at[k], dev(z, at_y(sides[k][1]), 1, t)
            )
        share(0)
        for k in range(2):
            yy = at_y(-sides[k][1])
            arrived(column(yy), fy_recv.at[k], fy_send.at[k])
            send(
                pending, half_column(yy, k), half_column(yy, k), fr_send.at[k], fr_recv.at[k],
                dev(z, at_y(sides[k][1]), 1, t),
            )
            share(3 if k == 0 else 1)
        for k in range(2):
            arrived(half_column(at_y(2), k), fr_recv.at[k], fr_send.at[k])
        share(2)
        own_copy.wait()
        arrived(kept(z, y, 0), ss_recv.at[0, 0], ss_send.at[0, 0])
        for rel in range(NZ):
            for d in range(NY):
                if rel or d:
                    arrived(chunk(at_z(rel), at_y(d)), ss_recv.at[rel, d], ss_send.at[rel, d])
        for copy in pending:
            copy.wait_send()

    for copy in started:
        copy.wait_send()


PAIR = 2


def attend_kernel(owner_ref, chosen_ref, *refs):
    blocks, (cos_ref, sin_ref, q_ref, own_ref, out_ref), scratch = refs[:8], refs[8:13], refs[13:]
    kbufs, vbufs, sbufs, pbufs = scratch[0:2], scratch[2:4], scratch[4:6], scratch[6:8]
    col = lax.broadcasted_iota(jnp.int32, (CHUNK, 128), 1)
    token = lax.rem(lax.broadcasted_iota(jnp.int32, (CHUNK, 128), 0), QLEN)
    tail = jnp.where(col <= token, jnp.float32(0.0), jnp.float32(NEG))

    def turn(block, j):
        wide = block.astype(jnp.float32)
        wide = wide * cos_ref[j : j + 1, :] + pltpu.roll(wide, HD // 2, 1) * sin_ref[j : j + 1, :]
        return wide.astype(jnp.bfloat16)

    for i in range(PAIR):
        kbuf, vbuf = kbufs[i], vbufs[i]
        for j in range(SLOTS):
            block = blocks[i * SLOTS + j]
            keys = block[0, :, :HD]
            kbuf[j * PLEN : (j + 1) * PLEN, :] = turn(keys, j) if j else keys
            vbuf[j * PLEN : (j + 1) * PLEN, :] = block[0, :, HD:]
        kbuf[LAST : LAST + QLEN, :] = own_ref[i, :, :HD]
        vbuf[LAST : LAST + QLEN, :] = own_ref[i, :, HD:]
        kbuf[LAST + QLEN :, :] = jnp.zeros((128 - QLEN, HD), jnp.bfloat16)
        vbuf[LAST + QLEN :, :] = jnp.zeros((128 - QLEN, HD), jnp.bfloat16)
    for i in range(PAIR):
        query = q_ref[i]
        query = jnp.concatenate([query[:, h * HD : (h + 1) * HD] for h in range(GROUP)], 0)
        sbufs[i][...] = lax.dot_general(
            query, kbufs[i][...], (((1,), (1,)), ((), ())), preferred_element_type=jnp.float32
        )
    for i in range(PAIR):
        sbuf, pbuf = sbufs[i], pbufs[i]
        for first in range(0, GROUP * QLEN, CHUNK):
            rows = slice(first, first + CHUNK)
            raw = jnp.concatenate([sbuf[rows, :LAST], sbuf[rows, LAST:] + tail], 1)
            expo = jnp.exp2((raw - jnp.max(raw, 1, keepdims=True)) * SCALE)
            pbuf[rows, :] = (expo * (1.0 / jnp.sum(expo, 1, keepdims=True))).astype(jnp.bfloat16)
        result = jnp.dot(pbuf[...], vbufs[i][...], preferred_element_type=jnp.float32).astype(jnp.bfloat16)
        for h in range(GROUP):
            out_ref[i, :, h * HD : (h + 1) * HD] = result[h * QLEN : (h + 1) * QLEN]


def gather(stale, fresh_input, kv_weight, sel_index, cosine, sine):
    any_spec = pl.BlockSpec(memory_space=pl.ANY)
    dma = pltpu.SemaphoreType.DMA
    return pl.pallas_call(
        gather_kernel,
        out_shape=jax.ShapeDtypeStruct((NZ, NY, 2, PLEN, KV), jnp.bfloat16),
        in_specs=[any_spec] * 6,
        out_specs=any_spec,
        scratch_shapes=[
            pltpu.VMEM((PLEN, KV), jnp.bfloat16),
            pltpu.VMEM((KEPT, KV), jnp.bfloat16),
            pltpu.VMEM((2, SEL, KV), jnp.bfloat16),
            pltpu.VMEM((8, 2, SEL, 8 * HD), jnp.bfloat16),
            pltpu.VMEM((NY, 2, HD, KV), jnp.bfloat16),
            pltpu.VMEM((NZ, 2, SEL, KV), jnp.float32),
            pltpu.VMEM((NZ, 2, SEL, KV), jnp.float32),
            pltpu.VMEM((2, SEL, HD), jnp.float32),
            pltpu.VMEM((2, SEL, HD), jnp.float32),
            pltpu.VMEM((NY, 2, SEL, HD), jnp.bfloat16),
            pltpu.VMEM((HD, KV), jnp.bfloat16),
            pltpu.VMEM(cosine.shape, jnp.float32),
            pltpu.VMEM(sine.shape, jnp.float32),
            pltpu.SMEM((SEL, 64), jnp.int32),
            dma((12,)),
            dma((8,)), dma((8, 2)),
            dma((NX,)), dma((NX,)),
            dma((3,)), dma((3, 2)),
            dma((2,)), dma((2,)),
            dma((4,)), dma((4, 2)),
            dma((2,)), dma((2,)),
            dma((2, 5, NY)), dma((2, 5, NY)),
            dma((NZ, NY)), dma((NZ, NY)),
            dma((NZ,)), dma((NZ,)),
            dma((NZ,)), dma((NZ,)),
            dma((2,)), dma((2,)),
            dma((2,)), dma((2,)),
            dma((NY,)), dma((NY,)),
        ],
        compiler_params=pltpu.CompilerParams(
            collective_id=0, has_side_effects=True, vmem_limit_bytes=62 * 1024 * 1024
        ),
    )(
        stale,
        fresh_input.reshape(NY, 2, SEL, HD),
        kv_weight,
        sel_index.T,
        cosine,
        sine,
    )


def attend(owner, retrieval, passages, cosine, sine, queries, question_kv):
    def block_spec(k):
        i, j = k // SLOTS, k % SLOTS

        def place(step, owner_ref, chosen_ref):
            o = owner_ref[chosen_ref[j, PAIR * step + i]]
            return o, 0, 0

        return pl.BlockSpec((1, PLEN, KV), place)

    def by_pair(shape):
        return pl.BlockSpec((PAIR,) + shape[1:], lambda step, a, b: (step, 0, 0))

    def whole(shape):
        return pl.BlockSpec(shape, lambda step, a, b: (0, 0))

    rows = GROUP * QLEN
    return pl.pallas_call(
        attend_kernel,
        grid_spec=pltpu.PrefetchScalarGridSpec(
            num_scalar_prefetch=2,
            grid=(queries.shape[0] // PAIR,),
            in_specs=[block_spec(k) for k in range(PAIR * SLOTS)]
            + [whole(cosine.shape), whole(sine.shape), by_pair(queries.shape), by_pair(question_kv.shape)],
            out_specs=by_pair(queries.shape),
            scratch_shapes=[pltpu.VMEM((KEYS, HD), jnp.bfloat16)] * 4
            + [pltpu.VMEM((rows, KEYS), jnp.float32)] * 2
            + [pltpu.VMEM((rows, KEYS), jnp.bfloat16)] * 2,
        ),
        out_shape=jax.ShapeDtypeStruct(queries.shape, jnp.bfloat16),
        compiler_params=pltpu.CompilerParams(vmem_limit_bytes=62 * 1024 * 1024),
    )(owner, retrieval.T, *([passages] * (PAIR * SLOTS)), cosine, sine, queries, question_kv)


def local(stale, fresh_input, kv_weight, sel_index, owner, retrieval, queries, question_kv):
    cosine, sine = trig_tables()
    passages = gather(
        stale, fresh_input, kv_weight, sel_index, jnp.asarray(cosine[:PLEN]), jnp.asarray(sine[:PLEN])
    )
    return attend(
        owner, retrieval, passages.reshape(64, PLEN, KV), jnp.asarray(cosine[PLEN:]), jnp.asarray(sine[PLEN:]),
        queries, question_kv,
    )


def solution(mesh):
    return jax.shard_map(
        local,
        mesh=mesh,
        in_specs=(
            P("req", None, "tp"),
            P("tp", None, "req"),
            P("req", None),
            P(),
            P(),
            P("req", None),
            P("req", None, "tp"),
            P("req", None, "tp"),
        ),
        out_specs=P("req", None, "tp"),
        check_vma=False,
    )
```

time: 380 us -> 62 us (0.16); the launches traced: 373 us -> 61.8 us
  blocking collectives: 295 us -> 0 us
  Pallas kernels: 0 us -> 61.8 us
  local copies, waits for them, and re-layouts: 31.1 us -> 0 us
  between operations: 13.5 us -> 0.01 us
  matrix products: 11.6 us -> 0 us
  other arithmetic: 10.4 us -> 0 us
  waiting for transfers between devices: 7.33 us -> 0 us
  starting transfers between devices: 4.01 us -> 0 us
    psum x1 -> x0, blocking collectives: 295 us -> none  [local(): summed = lax.psum(partial_kv, 'req').astype(jnp.bfloat16)]
    pallas_call x0 -> x2, Pallas kernels: none -> 61.8 us  [the longest x1 54.7 us: gather(): pl.pallas_call(gather_kernel, out_shape=jax.ShapeDtypeStruct((NZ, NY, 2,...]
    dot_general x6 -> x0, matrix products: 11.6 us -> none  [the longest x1 7.13 us: blend_all(): jnp.einsum('psl,psc->plc', onehot.astype(jnp.bfloat16), fresh_rot, prefer...]
    unnamed x15 -> x0, local copies, waits for them, and re-layouts: 11 us -> none
    convert_element_type x7 -> x0, local copies, waits for them, and re-layouts: 8.88 us -> none  [the longest x1 4.18 us: local(): summed = lax.psum(partial_kv, 'req').astype(jnp.bfloat16)]
    gather x10 -> x0, local copies, waits for them, and re-layouts: 7.86 us -> none  [one_request(): rows = jnp.take(blended, jnp.take(owner, chosen), axis=0)]
    all_to_all x1 -> x0, waiting for transfers between devices: 6.6 us -> none  [local(): lax.all_to_all(summed, 'tp', split_axis=2, concat_axis=0, tiled=True)]
    another operation x5 -> x0, other arithmetic: 4.58 us -> none
  transfers between devices with their start and end apart: 2 -> 0, of which waited for: 1 -> 0; matrix products, arithmetic and copies ran while one was open for 7% -> 0% of each run, Pallas kernels for 0% -> 0%
where the time goes in v2:
time: 62 us; the launch traced here: 61.8 us
  Pallas kernels  61.8 us (100%)
    pallas_call x1, Pallas kernels, gather(): pl.pallas_call(gather_kernel, out_shape=jax.ShapeDtypeStruct((NZ, NY, 2,...  54.7 us
    pallas_call x1, Pallas kernels, attend(): pl.pallas_call(attend_kernel, grid_spec=pltpu.PrefetchScalarGridSpec(num_...  7.05 us

profile of v2, /device:TPU:1, one launch (start us, length us, event | category | flops | bytes accessed | tf_op | source)
XLA Modules:
  0.0 61.8 jit_solution(3556384180919889230)
XLA Ops:
  0.0 54.7 %shard_map.118 = bf16[8,4,2,128,256]{4,3,2,1,0:T(8,128)(2,1)} custom-call(bf16[1,128,256]{2,1,0:T(8,128)(2,1)} %stale_hbm.1, bf16[4,2,16,128]{3,2,1,0:T(8,128)(2,1)} %bitcast.12, bf16[128,2048]{1,0:T(8,128)(2,1)} %w_hbm.1, s32[16,64]{1,0:T(8,128)} %bitcast.13, f32[128,128]{1,0:T(8,128)} %constant.8.clone.cos_hbm, f32[128,128]{1,0:T(8,128)} %constant.9.clone.sin_hbm), custom_call_target="tpu_custom_call" | custom-call | tf_op jit(solution)/shard_map/pallas_call | solution.py:402
  54.7 7.0 %shard_map.119 = bf16[8,32,1024]{2,1,0:T(8,128)(2,1)} custom-call(s32[64]{0:T(128)} %owner_ref.1, s32[4,8]{1,0:T(4,128)} %bitcast.14, bf16[64,128,256]{2,1,0:T(8,128)(2,1)} %bitcast.4, bf16[64,128,256]{2,1,0:T(8,128)(2,1)} %bitcast.5, bf16[64,128,256]{2,1,0:T(8,128)(2,1)} %bitcast.6, bf16[64,128,256]{2,1,0:T(8,128)(2,1)} %bitcast.7, ...), custom_call_target="tpu_custom_call" | custom-call | tf_op jit(solution)/shard_map/pallas_call | solution.py:467

commit v3 on v2

--- a/solution.py
+++ b/solution.py
@@ -22,6 +22,7 @@
 SCALE = math.log2(math.e) / math.sqrt(HD)
 NEG = -1e30
 THETA = 500000.0
+PAIR = 2
 
 
 def trig_tables():
@@ -35,13 +36,14 @@
     )
 
 
-def gather_kernel(
-    stale_hbm, x_hbm, w_hbm, sel_hbm, cos_hbm, sin_hbm,
-    pas,
+def kernel(
+    stale_hbm, x_hbm, w_hbm, sel_hbm, cos_hbm, sin_hbm, owner_hbm, chosen_hbm, q_hbm, own_hbm,
+    out_hbm,
+    pas, kbuf0, vbuf0, kbuf1, vbuf1, sbuf0, pbuf0, sbuf1, pbuf1, q_ref, own_ref, out_ref, owner_ref, chosen_ref,
     stale_ref, own_rows, own_fresh, xbuf, wbuf, zsum, zrecv, trig_c, trig_s, x_ref, w_ref, cos_ref, sin_ref, sel_ref,
     local_sem, xy_send, xy_recv, xx_send, xx_recv, w_send, w_recv, wr_send, wr_recv,
     seed_send, seed_recv, yr_send, yr_recv, sz_send, sz_recv, ss_send, ss_recv,
-    rz_send, rz_recv, fz_send, fz_recv, fy_send, fy_recv, fr_send, fr_recv, fs_send, fs_recv,
+    rz_send, rz_recv, fz_send, fz_recv, fy_send, fy_recv, fr_send, fr_recv, fs_send, fs_recv, q_sem, out_sem,
 ):
     r, t = lax.axis_index("req"), lax.axis_index("tp")
     z, y, c = r // 8, lax.rem(r, 8) // 2, lax.rem(r, 2)
@@ -139,6 +141,12 @@
     load_w = load(w_hbm.at[:, columns], w_ref)
     load_cos = load(cos_hbm, cos_ref)
     load_sin = load(sin_hbm, sin_ref)
+    load_owner = load(owner_hbm, owner_ref)
+    load_chosen = load(chosen_hbm, chosen_ref)
+    later = []
+    for k, (source, target) in enumerate(((q_hbm, q_ref), (own_hbm, own_ref))):
+        later.append(pltpu.make_async_copy(source, target, q_sem.at[k]))
+        later[-1].start()
 
     load_sel.wait()
     lane = lax.broadcasted_iota(jnp.int32, (8, PLEN), 1)
@@ -160,6 +168,8 @@
     load_w.wait()
     load_cos.wait()
     load_sin.wait()
+    load_owner.wait()
+    load_chosen.wait()
 
     @pl.when(c == 0)
     def _():
@@ -351,60 +361,89 @@
     for copy in started:
         copy.wait_send()
 
-
-PAIR = 2
-
-
-def attend_kernel(owner_ref, chosen_ref, *refs):
-    blocks, (cos_ref, sin_ref, q_ref, own_ref, out_ref), scratch = refs[:8], refs[8:13], refs[13:]
-    kbufs, vbufs, sbufs, pbufs = scratch[0:2], scratch[2:4], scratch[4:6], scratch[6:8]
+    kbufs, vbufs, sbufs, pbufs = (kbuf0, kbuf1), (vbuf0, vbuf1), (sbuf0, sbuf1), (pbuf0, pbuf1)
+    steps = q_ref.shape[0] // PAIR
+
+    def result_copy(step):
+        rows = pl.ds(step * PAIR, PAIR)
+        return pltpu.make_async_copy(out_ref.at[rows], out_hbm.at[rows], out_sem.at[step])
+
     col = lax.broadcasted_iota(jnp.int32, (CHUNK, 128), 1)
     token = lax.rem(lax.broadcasted_iota(jnp.int32, (CHUNK, 128), 0), QLEN)
     tail = jnp.where(col <= token, jnp.float32(0.0), jnp.float32(NEG))
+    for i in range(PAIR):
+        kbufs[i][LAST + QLEN :, :] = jnp.zeros((128 - QLEN, HD), jnp.bfloat16)
+        vbufs[i][LAST + QLEN :, :] = jnp.zeros((128 - QLEN, HD), jnp.bfloat16)
+    for copy in later:
+        copy.wait()
 
     def turn(block, j):
         wide = block.astype(jnp.float32)
-        wide = wide * cos_ref[j : j + 1, :] + pltpu.roll(wide, HD // 2, 1) * sin_ref[j : j + 1, :]
+        wide = wide * cos_ref[PLEN + j : PLEN + j + 1, :] + pltpu.roll(wide, HD // 2, 1) * sin_ref[PLEN + j : PLEN + j + 1, :]
         return wide.astype(jnp.bfloat16)
 
-    for i in range(PAIR):
-        kbuf, vbuf = kbufs[i], vbufs[i]
-        for j in range(SLOTS):
-            block = blocks[i * SLOTS + j]
-            keys = block[0, :, :HD]
-            kbuf[j * PLEN : (j + 1) * PLEN, :] = turn(keys, j) if j else keys
-            vbuf[j * PLEN : (j + 1) * PLEN, :] = block[0, :, HD:]
-        kbuf[LAST : LAST + QLEN, :] = own_ref[i, :, :HD]
-        vbuf[LAST : LAST + QLEN, :] = own_ref[i, :, HD:]
-        kbuf[LAST + QLEN :, :] = jnp.zeros((128 - QLEN, HD), jnp.bfloat16)
-        vbuf[LAST + QLEN :, :] = jnp.zeros((128 - QLEN, HD), jnp.bfloat16)
-    for i in range(PAIR):
-        query = q_ref[i]
-        query = jnp.concatenate([query[:, h * HD : (h + 1) * HD] for h in range(GROUP)], 0)
-        sbufs[i][...] = lax.dot_general(
-            query, kbufs[i][...], (((1,), (1,)), ((), ())), preferred_element_type=jnp.float32
-        )
-    for i in range(PAIR):
-        sbuf, pbuf = sbufs[i], pbufs[i]
-        for first in range(0, GROUP * QLEN, CHUNK):
-            rows = slice(first, first + CHUNK)
-            raw = jnp.concatenate([sbuf[rows, :LAST], sbuf[rows, LAST:] + tail], 1)
-            expo = jnp.exp2((raw - jnp.max(raw, 1, keepdims=True)) * SCALE)
-            pbuf[rows, :] = (expo * (1.0 / jnp.sum(expo, 1, keepdims=True))).astype(jnp.bfloat16)
-        result = jnp.dot(pbuf[...], vbufs[i][...], preferred_element_type=jnp.float32).astype(jnp.bfloat16)
-        for h in range(GROUP):
-            out_ref[i, :, h * HD : (h + 1) * HD] = result[h * QLEN : (h + 1) * QLEN]
-
-
-def gather(stale, fresh_input, kv_weight, sel_index, cosine, sine):
+    def pair(step, carry):
+        for i in range(PAIR):
+            kbuf, vbuf = kbufs[i], vbufs[i]
+            request = step * PAIR + i
+            for j in range(SLOTS):
+                o = owner_ref[chosen_ref[j, request]]
+                block = pas[o // 8, lax.rem(o, 8) // 2, lax.rem(o, 2)]
+                keys = block[:, :HD]
+                kbuf[j * PLEN : (j + 1) * PLEN, :] = turn(keys, j) if j else keys
+                vbuf[j * PLEN : (j + 1) * PLEN, :] = block[:, HD:]
+            own = own_ref[request]
+            kbuf[LAST : LAST + QLEN, :] = own[:, :HD]
+            vbuf[LAST : LAST + QLEN, :] = own[:, HD:]
+        for i in range(PAIR):
+            query = q_ref[step * PAIR + i]
+            query = jnp.concatenate([query[:, h * HD : (h + 1) * HD] for h in range(GROUP)], 0)
+            sbufs[i][...] = lax.dot_general(
+                query, kbufs[i][...], (((1,), (1,)), ((), ())), preferred_element_type=jnp.float32
+            )
+        for i in range(PAIR):
+            sbuf, pbuf = sbufs[i], pbufs[i]
+            for first in range(0, GROUP * QLEN, CHUNK):
+                rows = slice(first, first + CHUNK)
+                raw = jnp.concatenate([sbuf[rows, :LAST], sbuf[rows, LAST:] + tail], 1)
+                expo = jnp.exp2((raw - jnp.max(raw, 1, keepdims=True)) * SCALE)
+                pbuf[rows, :] = (expo * (1.0 / jnp.sum(expo, 1, keepdims=True))).astype(jnp.bfloat16)
+            result = jnp.dot(pbuf[...], vbufs[i][...], preferred_element_type=jnp.float32).astype(jnp.bfloat16)
+            for h in range(GROUP):
+                out_ref[step * PAIR + i, :, h * HD : (h + 1) * HD] = result[h * QLEN : (h + 1) * QLEN]
+        result_copy(step).start()
+        return carry
+
+    lax.fori_loop(0, steps, pair, 0)
+    for step in range(steps):
+        result_copy(step).wait()
+
+
+def local(stale, fresh_input, kv_weight, sel_index, owner, retrieval, queries, question_kv):
+    cosine, sine = trig_tables()
     any_spec = pl.BlockSpec(memory_space=pl.ANY)
     dma = pltpu.SemaphoreType.DMA
+    rows = GROUP * QLEN
     return pl.pallas_call(
-        gather_kernel,
-        out_shape=jax.ShapeDtypeStruct((NZ, NY, 2, PLEN, KV), jnp.bfloat16),
-        in_specs=[any_spec] * 6,
+        kernel,
+        out_shape=jax.ShapeDtypeStruct(queries.shape, jnp.bfloat16),
+        in_specs=[any_spec] * 10,
         out_specs=any_spec,
         scratch_shapes=[
+            pltpu.VMEM((NZ, NY, 2, PLEN, KV), jnp.bfloat16),
+            pltpu.VMEM((KEYS, HD), jnp.bfloat16),
+            pltpu.VMEM((KEYS, HD), jnp.bfloat16),
+            pltpu.VMEM((KEYS, HD), jnp.bfloat16),
+            pltpu.VMEM((KEYS, HD), jnp.bfloat16),
+            pltpu.VMEM((rows, KEYS), jnp.float32),
+            pltpu.VMEM((rows, KEYS), jnp.bfloat16),
+            pltpu.VMEM((rows, KEYS), jnp.float32),
+            pltpu.VMEM((rows, KEYS), jnp.bfloat16),
+            pltpu.VMEM(queries.shape, jnp.bfloat16),
+            pltpu.VMEM(question_kv.shape, jnp.bfloat16),
+            pltpu.VMEM(queries.shape, jnp.bfloat16),
+            pltpu.SMEM((64,), jnp.int32),
+            pltpu.SMEM((SLOTS, 8), jnp.int32),
             pltpu.VMEM((PLEN, KV), jnp.bfloat16),
             pltpu.VMEM((KEPT, KV), jnp.bfloat16),
             pltpu.VMEM((2, SEL, KV), jnp.bfloat16),
@@ -433,6 +472,7 @@
             dma((2,)), dma((2,)),
             dma((2,)), dma((2,)),
             dma((NY,)), dma((NY,)),
+            dma((2,)), dma((4,)),
         ],
         compiler_params=pltpu.CompilerParams(
             collective_id=0, has_side_effects=True, vmem_limit_bytes=62 * 1024 * 1024
@@ -442,53 +482,12 @@
         fresh_input.reshape(NY, 2, SEL, HD),
         kv_weight,
         sel_index.T,
-        cosine,
-        sine,
-    )
-
-
-def attend(owner, retrieval, passages, cosine, sine, queries, question_kv):
-    def block_spec(k):
-        i, j = k // SLOTS, k % SLOTS
-
-        def place(step, owner_ref, chosen_ref):
-            o = owner_ref[chosen_ref[j, PAIR * step + i]]
-            return o, 0, 0
-
-        return pl.BlockSpec((1, PLEN, KV), place)
-
-    def by_pair(shape):
-        return pl.BlockSpec((PAIR,) + shape[1:], lambda step, a, b: (step, 0, 0))
-
-    def whole(shape):
-        return pl.BlockSpec(shape, lambda step, a, b: (0, 0))
-
-    rows = GROUP * QLEN
-    return pl.pallas_call(
-        attend_kernel,
-        grid_spec=pltpu.PrefetchScalarGridSpec(
-            num_scalar_prefetch=2,
-            grid=(queries.shape[0] // PAIR,),
-            in_specs=[block_spec(k) for k in range(PAIR * SLOTS)]
-            + [whole(cosine.shape), whole(sine.shape), by_pair(queries.shape), by_pair(question_kv.shape)],
-            out_specs=by_pair(queries.shape),
-            scratch_shapes=[pltpu.VMEM((KEYS, HD), jnp.bfloat16)] * 4
-            + [pltpu.VMEM((rows, KEYS), jnp.float32)] * 2
-            + [pltpu.VMEM((rows, KEYS), jnp.bfloat16)] * 2,
-        ),
-        out_shape=jax.ShapeDtypeStruct(queries.shape, jnp.bfloat16),
-        compiler_params=pltpu.CompilerParams(vmem_limit_bytes=62 * 1024 * 1024),
-    )(owner, retrieval.T, *([passages] * (PAIR * SLOTS)), cosine, sine, queries, question_kv)
-
-
-def local(stale, fresh_input, kv_weight, sel_index, owner, retrieval, queries, question_kv):
-    cosine, sine = trig_tables()
-    passages = gather(
-        stale, fresh_input, kv_weight, sel_index, jnp.asarray(cosine[:PLEN]), jnp.asarray(sine[:PLEN])
-    )
-    return attend(
-        owner, retrieval, passages.reshape(64, PLEN, KV), jnp.asarray(cosine[PLEN:]), jnp.asarray(sine[PLEN:]),
-        queries, question_kv,
+        jnp.asarray(cosine),
+        jnp.asarray(sine),
+        owner,
+        retrieval.T,
+        queries,
+        question_kv,
     )
 
 

time: 62 us -> 60 us (0.968)
  Pallas kernels: 61.8 us -> 57.9 us
  local copies, waits for them, and re-layouts: 0 us -> 1.87 us
    pallas_call x2 -> x1, Pallas kernels: 61.8 us -> 57.9 us  [local(): pl.pallas_call(kernel, out_shape=jax.ShapeDtypeStruct(queries.shape, jnp....]
    unnamed x0 -> x1, local copies, waits for them, and re-layouts: none -> 1.87 us
where the time goes in v3:
time: 60 us; the launch traced here: 59.8 us
  Pallas kernels  57.9 us (96%)
  local copies, waits for them, and re-layouts  1.87 us (3%)
    pallas_call x1, Pallas kernels, local(): pl.pallas_call(kernel, out_shape=jax.ShapeDtypeStruct(queries.shape, jnp....  57.9 us
    unnamed x1, local copies, waits for them, and re-layouts  1.87 us

profile of v3, /device:TPU:1, one launch (start us, length us, event | category | flops | bytes accessed | tf_op | source)
XLA Modules:
  0.0 59.8 jit_solution(9379305952710785170)
XLA Ops:
  0.0 57.9 %shard_map.100 = bf16[8,32,1024]{2,1,0:T(8,128)(2,1)} custom-call(bf16[1,128,256]{2,1,0:T(8,128)(2,1)} %stale_hbm.1, bf16[4,2,16,128]{3,2,1,0:T(8,128)(2,1)} %bitcast.3, bf16[128,2048]{1,0:T(8,128)(2,1)} %w_hbm.1, s32[16,64]{1,0:T(8,128)} %bitcast.4, f32[136,128]{1,0:T(8,128)} %constant.4.clone.cos_hbm, f32[136,128]{1,0:T(8,128)} %constant.5.clone.sin_hbm, ...), custom_call_target="tpu_custom_call" | custom-call | tf_op jit(solution)/shard_map/pallas_call | solution.py:427
  58.0 1.9 %copy.12 = bf16[8,32,1024]{2,1,0:T(8,128)(2,1)} copy(bf16[8,32,1024]{2,1,0:T(8,128)(2,1)} %shard_map.100) | data formatting | bytes 1048576

commit v4 on v3

--- a/solution.py
+++ b/solution.py
@@ -42,7 +42,7 @@
     pas, kbuf0, vbuf0, kbuf1, vbuf1, sbuf0, pbuf0, sbuf1, pbuf1, q_ref, own_ref, out_ref, owner_ref, chosen_ref,
     stale_ref, own_rows, own_fresh, xbuf, wbuf, zsum, zrecv, trig_c, trig_s, x_ref, w_ref, cos_ref, sin_ref, sel_ref,
     local_sem, xy_send, xy_recv, xx_send, xx_recv, w_send, w_recv, wr_send, wr_recv,
-    seed_send, seed_recv, yr_send, yr_recv, sz_send, sz_recv, ss_send, ss_recv,
+    seed_send, seed_recv, yr_send, yr_recv, yf_send, yf_recv, sz_send, sz_recv, ss_send, ss_recv,
     rz_send, rz_recv, fz_send, fz_recv, fy_send, fy_recv, fr_send, fr_recv, fs_send, fs_recv, q_sem, out_sem,
 ):
     r, t = lax.axis_index("req"), lax.axis_index("tp")
@@ -115,11 +115,11 @@
     def column(yy):
         return pas.at[:, yy, :, pl.ds(KEPT, SEL)]
 
-    def half_column(yy, cc):
-        return pas.at[:, yy, cc, pl.ds(KEPT, SEL)]
-
-    def fresh_slot(zz):
-        return pas.at[zz, y, :, pl.ds(KEPT, SEL)]
+    def piece(zz, yy):
+        return pas.at[zz, yy, :, pl.ds(KEPT, SEL)]
+
+    def half_piece(zz, yy, cc):
+        return pas.at[zz, yy, cc, pl.ds(KEPT, SEL)]
 
     def xpiece(ts, ys, cs):
         return xbuf.at[ts, :, :, pl.ds(pl.multiple_of((ys * 2 + cs) * HD, HD), HD)]
@@ -219,9 +219,12 @@
                 ring(z, at_y(d), 1, d, way)
             share(z, at_y(d), 0, d)
 
+        def last_way(d):
+            return 0 if d == 1 else 1
+
         def hop(s, d):
             for way in range(2):
-                if s == 4 and (d < 2) != (way == 0):
+                if s == 4 and way != last_way(d):
                     continue
                 rel = (-s if way == 0 else s) % NZ
                 zz, yy = at_z(rel), at_y(d)
@@ -230,8 +233,14 @@
                         arrived(kept(zz, yy, cc), seed_recv.at[2 + way, cc], seed_send.at[2 + way])
                 else:
                     arrived(chunk(zz, yy), sz_recv.at[way, s, d], sz_send.at[way, s, d])
-                if s < 3 or (s == 3 and (d < 2) == (way == 0)):
+                if s < (2 if d == 2 else 3) or (s == 3 and way == last_way(d)):
                     ring(zz, yy, s + 1, d, way)
+                if s >= 3 and d:
+                    k = 0 if d == 3 else 1
+                    send(
+                        pending, kept(zz, yy, k), kept(zz, yy, k), yf_send.at[rel, k], yf_recv.at[rel, k],
+                        dev(z, at_y(sides[k][1]), 0, t),
+                    )
                 share(zz, yy, rel, d)
 
         hop(1, 0)
@@ -254,9 +263,13 @@
         arrived(kept(z, y, 1), ss_recv.at[0, 0], ss_send.at[0, 0])
         send(pending, kept(z, y, 0), kept(z, y, 0), ss_send.at[0, 0], ss_recv.at[0, 0], mate)
         for s, d in (
-            (3, 0), (2, 3), (2, 1), (1, 2), (4, 0), (3, 3), (3, 1), (2, 2), (4, 3), (4, 1), (3, 2), (4, 2),
+            (3, 0), (2, 3), (2, 1), (1, 2), (4, 0), (3, 3), (3, 1), (2, 2), (4, 3), (4, 1),
         ):
             hop(s, d)
+        for rel in (5, 3, 4):
+            for k in range(2):
+                arrived(kept(at_z(rel), at_y(2), k), yf_recv.at[rel, k], yf_send.at[rel, k])
+            share(at_z(rel), at_y(2), rel, 2)
         for d in range(NY):
             arrived(column(at_y(d)), fs_recv.at[d], fs_send.at[d])
         for copy in pending:
@@ -323,31 +336,38 @@
             own_fresh[cc, :, :HD] = keys.astype(jnp.bfloat16)
             own_fresh[cc, :, HD:] = fresh[cc, :, HD:].astype(jnp.bfloat16)
         for k in range(1, NZ):
-            send(pending, own_fresh, fresh_slot(z), fz_send.at[k], fz_recv.at[k], dev(at_z(k), y, 1, t))
-        keep_fresh = pltpu.make_async_copy(own_fresh, fresh_slot(z), local_sem.at[len(loads) + 3])
+            send(pending, own_fresh, piece(z, y), fz_send.at[k], fz_recv.at[k], dev(at_z(k), y, 1, t))
+        keep_fresh = pltpu.make_async_copy(own_fresh, piece(z, y), local_sem.at[len(loads) + 3])
         keep_fresh.start()
         keep_fresh.wait()
-        for k in range(1, NZ):
-            arrived(fresh_slot(at_z(-k)), fz_recv.at[k], fz_send.at[k])
-
         def share(d):
             send(pending, column(at_y(d)), column(at_y(d)), fs_send.at[d], fs_recv.at[d], mate)
 
-        for k in range(2):
-            send(
-                pending, column(y), column(y), fy_send.at[k], fy_recv.at[k], dev(z, at_y(sides[k][1]), 1, t)
-            )
+        near_first = (0, 1, 7, 2, 6, 3, 5, 4)
+        for rel in near_first:
+            here = piece(at_z(-rel), y)
+            if rel:
+                arrived(here, fz_recv.at[rel], fz_send.at[rel])
+            for k in range(2):
+                send(
+                    pending, here, here, fy_send.at[rel, k], fy_recv.at[rel, k],
+                    dev(z, at_y(sides[k][1]), 1, t),
+                )
         share(0)
-        for k in range(2):
-            yy = at_y(-sides[k][1])
-            arrived(column(yy), fy_recv.at[k], fy_send.at[k])
-            send(
-                pending, half_column(yy, k), half_column(yy, k), fr_send.at[k], fr_recv.at[k],
-                dev(z, at_y(sides[k][1]), 1, t),
-            )
-            share(3 if k == 0 else 1)
-        for k in range(2):
-            arrived(half_column(at_y(2), k), fr_recv.at[k], fr_send.at[k])
+        for rel in near_first:
+            zz = at_z(-rel)
+            for k in range(2):
+                yy = at_y(-sides[k][1])
+                arrived(piece(zz, yy), fy_recv.at[rel, k], fy_send.at[rel, k])
+                send(
+                    pending, half_piece(zz, yy, k), half_piece(zz, yy, k), fr_send.at[rel, k], fr_recv.at[rel, k],
+                    dev(z, at_y(sides[k][1]), 1, t),
+                )
+        share(3)
+        share(1)
+        for rel in near_first:
+            for k in range(2):
+                arrived(half_piece(at_z(-rel), at_y(2), k), fr_recv.at[rel, k], fr_send.at[rel, k])
         share(2)
         own_copy.wait()
         arrived(kept(z, y, 0), ss_recv.at[0, 0], ss_send.at[0, 0])
@@ -465,12 +485,13 @@
             dma((2,)), dma((2,)),
             dma((4,)), dma((4, 2)),
             dma((2,)), dma((2,)),
+            dma((NZ, 2)), dma((NZ, 2)),
             dma((2, 5, NY)), dma((2, 5, NY)),
             dma((NZ, NY)), dma((NZ, NY)),
             dma((NZ,)), dma((NZ,)),
             dma((NZ,)), dma((NZ,)),
-            dma((2,)), dma((2,)),
-            dma((2,)), dma((2,)),
+            dma((NZ, 2)), dma((NZ, 2)),
+            dma((NZ, 2)), dma((NZ, 2)),
             dma((NY,)), dma((NY,)),
             dma((2,)), dma((4,)),
         ],

time: 60 us -> 58.1 us (0.968)
  Pallas kernels: 57.9 us -> 56 us
    pallas_call x1, Pallas kernels: 57.9 us -> 56 us  [local(): pl.pallas_call(kernel, out_shape=jax.ShapeDtypeStruct(queries.shape, jnp....]
where the time goes in v4:
time: 58.1 us; the launch traced here: 57.9 us
  Pallas kernels  56 us (96%)
  local copies, waits for them, and re-layouts  1.87 us (3%)
    pallas_call x1, Pallas kernels, local(): pl.pallas_call(kernel, out_shape=jax.ShapeDtypeStruct(queries.shape, jnp....  56 us
    unnamed x1, local copies, waits for them, and re-layouts  1.87 us

profile of v4, /device:TPU:1, one launch (start us, length us, event | category | flops | bytes accessed | tf_op | source)
XLA Modules:
  0.0 57.9 jit_solution(2013729452500189906)
XLA Ops:
  0.0 56.0 %shard_map.100 = bf16[8,32,1024]{2,1,0:T(8,128)(2,1)} custom-call(bf16[1,128,256]{2,1,0:T(8,128)(2,1)} %stale_hbm.1, bf16[4,2,16,128]{3,2,1,0:T(8,128)(2,1)} %bitcast.3, bf16[128,2048]{1,0:T(8,128)(2,1)} %w_hbm.1, s32[16,64]{1,0:T(8,128)} %bitcast.4, f32[136,128]{1,0:T(8,128)} %constant.4.clone.cos_hbm, f32[136,128]{1,0:T(8,128)} %constant.5.clone.sin_hbm, ...), custom_call_target="tpu_custom_call" | custom-call | tf_op jit(solution)/shard_map/pallas_call | solution.py:447
  56.0 1.9 %copy.12 = bf16[8,32,1024]{2,1,0:T(8,128)(2,1)} copy(bf16[8,32,1024]{2,1,0:T(8,128)(2,1)} %shard_map.100) | data formatting | bytes 1048576

commit v5 on v4

--- a/solution.py
+++ b/solution.py
@@ -148,6 +148,22 @@
         later.append(pltpu.make_async_copy(source, target, q_sem.at[k]))
         later[-1].start()
 
+    load_x.wait()
+
+    @pl.when(c == 0)
+    def _():
+        pl.semaphore_wait(barrier, 12)
+
+    @pl.when(c == 1)
+    def _():
+        pl.semaphore_wait(barrier, 22)
+
+    started = []
+    for k, (dy, dl) in enumerate(line[1:]):
+        send(
+            started, x_ref.at[at_y(dy)], xpiece(t, y, c), xy_send.at[k + 1], xy_recv.at[k + 1, c],
+            dev(z, at_y(dy), 1, other(dl) * 4 + x),
+        )
     load_sel.wait()
     lane = lax.broadcasted_iota(jnp.int32, (8, PLEN), 1)
     hit = lane == sel_ref[0, r]
@@ -164,36 +180,19 @@
     picked = jnp.where(order == rank[0:1], keep[0:1], jnp.float32(0.0)).astype(jnp.bfloat16)
     load_stale.wait()
     own_rows[...] = jnp.dot(picked, stale_ref[...], preferred_element_type=jnp.float32).astype(jnp.bfloat16)
-    load_x.wait()
-    load_w.wait()
-    load_cos.wait()
-    load_sin.wait()
-    load_owner.wait()
-    load_chosen.wait()
-
-    @pl.when(c == 0)
-    def _():
-        pl.semaphore_wait(barrier, 12)
-
-    @pl.when(c == 1)
-    def _():
-        pl.semaphore_wait(barrier, 22)
-
-    started = []
-    for k, (dy, dl) in enumerate(line[1:]):
-        send(
-            started, x_ref.at[at_y(dy)], xpiece(t, y, c), xy_send.at[k + 1], xy_recv.at[k + 1, c],
-            dev(z, at_y(dy), 1, other(dl) * 4 + x),
-        )
     for k in (2, 3, 0, 1):
         dz, dy = sides[k]
         send(
             started, own_rows, kept(z, y, c), seed_send.at[k], seed_recv.at[k, c], dev(at_z(dz), at_y(dy), 0, t)
         )
+    load_w.wait()
     for k in range(2):
         send(
             started, w_ref, wpiece(y, c), w_send.at[k], w_recv.at[k, c], dev(z, at_y(sides[k][1]), 1, t)
         )
+
+    for copy in (load_cos, load_sin, load_owner, load_chosen):
+        copy.wait()
 
     @pl.when(c == 0)
     def _():
@@ -204,61 +203,63 @@
         own_copy = pltpu.make_async_copy(own_rows, kept(z, y, 0), local_sem.at[len(loads)])
         own_copy.start()
 
-        def ring(zz, yy, s, d, way):
+        def ring(zz, yy, s, d, way, cc):
             step = 1 if way == 0 else -1
             send(
-                pending, chunk(zz, yy), chunk(zz, yy), sz_send.at[way, s, d], sz_recv.at[way, s, d],
+                pending, kept(zz, yy, cc), kept(zz, yy, cc), sz_send.at[way, s, d, cc], sz_recv.at[way, s, d, cc],
                 dev(at_z(step), y, 0, t),
             )
 
         def share(zz, yy, rel, d):
             send(pending, chunk(zz, yy), chunk(zz, yy), ss_send.at[rel, d], ss_recv.at[rel, d], mate)
 
-        def inject(d):
+        def inject(d, cc):
             for way in range(2):
-                ring(z, at_y(d), 1, d, way)
-            share(z, at_y(d), 0, d)
+                ring(z, at_y(d), 1, d, way, cc)
 
         def last_way(d):
             return 0 if d == 1 else 1
 
         def hop(s, d):
-            for way in range(2):
-                if s == 4 and way != last_way(d):
-                    continue
-                rel = (-s if way == 0 else s) % NZ
-                zz, yy = at_z(rel), at_y(d)
-                if s == 1 and d == 0:
-                    for cc in range(2):
-                        arrived(kept(zz, yy, cc), seed_recv.at[2 + way, cc], seed_send.at[2 + way])
-                else:
-                    arrived(chunk(zz, yy), sz_recv.at[way, s, d], sz_send.at[way, s, d])
-                if s < (2 if d == 2 else 3) or (s == 3 and way == last_way(d)):
-                    ring(zz, yy, s + 1, d, way)
-                if s >= 3 and d:
-                    k = 0 if d == 3 else 1
-                    send(
-                        pending, kept(zz, yy, k), kept(zz, yy, k), yf_send.at[rel, k], yf_recv.at[rel, k],
-                        dev(z, at_y(sides[k][1]), 0, t),
-                    )
-                share(zz, yy, rel, d)
+            ways = [way for way in range(2) if s < 4 or way == last_way(d)]
+            where = [((-s if way == 0 else s) % NZ, way) for way in ways]
+            for cc in range(2):
+                for rel, way in where:
+                    block = kept(at_z(rel), at_y(d), cc)
+                    if s == 1 and d == 0:
+                        arrived(block, seed_recv.at[2 + way, cc], seed_send.at[2 + way])
+                    else:
+                        arrived(block, sz_recv.at[way, s, d, cc], sz_send.at[way, s, d, cc])
+                    if s < (2 if d == 2 else 3) or (s == 3 and way == last_way(d)):
+                        ring(at_z(rel), at_y(d), s + 1, d, way, cc)
+                    if s >= 3 and d and cc == (0 if d == 3 else 1):
+                        send(
+                            pending, block, block, yf_send.at[rel, cc], yf_recv.at[rel, cc],
+                            dev(z, at_y(sides[cc][1]), 0, t),
+                        )
+            for rel, way in where:
+                share(at_z(rel), at_y(d), rel, d)
 
         hop(1, 0)
         for k in range(2):
             yy = at_y(-sides[k][1])
+            d = 3 if k == 0 else 1
             for cc in range(2):
                 arrived(kept(z, yy, cc), seed_recv.at[k, cc], seed_send.at[k])
-            send(
-                pending, kept(z, yy, k), kept(z, yy, k), yr_send.at[k], yr_recv.at[k],
-                dev(z, at_y(sides[k][1]), 0, t),
-            )
-            inject(3 if k == 0 else 1)
+                if cc == k:
+                    send(
+                        pending, kept(z, yy, k), kept(z, yy, k), yr_send.at[k], yr_recv.at[k],
+                        dev(z, at_y(sides[k][1]), 0, t),
+                    )
+                inject(d, cc)
+            share(z, yy, 0, d)
         hop(2, 0)
         hop(1, 3)
         hop(1, 1)
         for k in range(2):
             arrived(kept(z, at_y(2), k), yr_recv.at[k], yr_send.at[k])
-        inject(2)
+            inject(2, k)
+        share(z, at_y(2), 0, 2)
         own_copy.wait()
         arrived(kept(z, y, 1), ss_recv.at[0, 0], ss_send.at[0, 0])
         send(pending, kept(z, y, 0), kept(z, y, 0), ss_send.at[0, 0], ss_recv.at[0, 0], mate)
@@ -321,7 +322,7 @@
             preferred_element_type=jnp.float32,
         )
         zsum[...] = part.reshape(NZ, 2, SEL, KV)
-        for k in range(1, NZ):
+        for k in (4, 3, 5, 2, 6, 1, 7):
             send(
                 pending, zsum.at[at_z(k)], zrecv.at[k], rz_send.at[k], rz_recv.at[k], dev(at_z(k), y, 1, t)
             )
@@ -335,7 +336,7 @@
             keys = keys * trig_c[cc] + pltpu.roll(keys, HD // 2, 1) * trig_s[cc]
             own_fresh[cc, :, :HD] = keys.astype(jnp.bfloat16)
             own_fresh[cc, :, HD:] = fresh[cc, :, HD:].astype(jnp.bfloat16)
-        for k in range(1, NZ):
+        for k in (1, 7, 2, 6, 3, 5, 4):
             send(pending, own_fresh, piece(z, y), fz_send.at[k], fz_recv.at[k], dev(at_z(k), y, 1, t))
         keep_fresh = pltpu.make_async_copy(own_fresh, piece(z, y), local_sem.at[len(loads) + 3])
         keep_fresh.start()
@@ -486,7 +487,7 @@
             dma((4,)), dma((4, 2)),
             dma((2,)), dma((2,)),
             dma((NZ, 2)), dma((NZ, 2)),
-            dma((2, 5, NY)), dma((2, 5, NY)),
+            dma((2, 5, NY, 2)), dma((2, 5, NY, 2)),
             dma((NZ, NY)), dma((NZ, NY)),
             dma((NZ,)), dma((NZ,)),
             dma((NZ,)), dma((NZ,)),

time: 58.1 us -> 59.2 us (1.019)
  Pallas kernels: 56 us -> 57.1 us
    pallas_call x1, Pallas kernels: 56 us -> 57.1 us  [local(): pl.pallas_call(kernel, out_shape=jax.ShapeDtypeStruct(queries.shape, jnp....]
where the time goes in v5:
time: 59.2 us; the launch traced here: 59 us
  Pallas kernels  57.1 us (96%)
  local copies, waits for them, and re-layouts  1.87 us (3%)
    pallas_call x1, Pallas kernels, local(): pl.pallas_call(kernel, out_shape=jax.ShapeDtypeStruct(queries.shape, jnp....  57.1 us
    unnamed x1, local copies, waits for them, and re-layouts  1.87 us

profile of v5, /device:TPU:1, one launch (start us, length us, event | category | flops | bytes accessed | tf_op | source)
XLA Modules:
  0.0 59.0 jit_solution(15864780813006829160)
XLA Ops:
  0.0 57.1 %shard_map.100 = bf16[8,32,1024]{2,1,0:T(8,128)(2,1)} custom-call(bf16[1,128,256]{2,1,0:T(8,128)(2,1)} %stale_hbm.1, bf16[4,2,16,128]{3,2,1,0:T(8,128)(2,1)} %bitcast.3, bf16[128,2048]{1,0:T(8,128)(2,1)} %w_hbm.1, s32[16,64]{1,0:T(8,128)} %bitcast.4, f32[136,128]{1,0:T(8,128)} %constant.4.clone.cos_hbm, f32[136,128]{1,0:T(8,128)} %constant.5.clone.sin_hbm, ...), custom_call_target="tpu_custom_call" | custom-call | tf_op jit(solution)/shard_map/pallas_call | solution.py:448
  57.2 1.9 %copy.12 = bf16[8,32,1024]{2,1,0:T(8,128)(2,1)} copy(bf16[8,32,1024]{2,1,0:T(8,128)(2,1)} %shard_map.100) | data formatting | bytes 1048576

commit v6 on v4

--- a/solution.py
+++ b/solution.py
@@ -147,6 +147,28 @@
     for k, (source, target) in enumerate(((q_hbm, q_ref), (own_hbm, own_ref))):
         later.append(pltpu.make_async_copy(source, target, q_sem.at[k]))
         later[-1].start()
+
+    load_x.wait()
+
+    @pl.when(c == 0)
+    def _():
+        pl.semaphore_wait(barrier, 12)
+
+    @pl.when(c == 1)
+    def _():
+        pl.semaphore_wait(barrier, 22)
+
+    started = []
+    for k, (dy, dl) in enumerate(line[1:]):
+        send(
+            started, x_ref.at[at_y(dy)], xpiece(t, y, c), xy_send.at[k + 1], xy_recv.at[k + 1, c],
+            dev(z, at_y(dy), 1, other(dl) * 4 + x),
+        )
+    load_w.wait()
+    for k in range(2):
+        send(
+            started, w_ref, wpiece(y, c), w_send.at[k], w_recv.at[k, c], dev(z, at_y(sides[k][1]), 1, t)
+        )
 
     load_sel.wait()
     lane = lax.broadcasted_iota(jnp.int32, (8, PLEN), 1)
@@ -164,36 +186,13 @@
     picked = jnp.where(order == rank[0:1], keep[0:1], jnp.float32(0.0)).astype(jnp.bfloat16)
     load_stale.wait()
     own_rows[...] = jnp.dot(picked, stale_ref[...], preferred_element_type=jnp.float32).astype(jnp.bfloat16)
-    load_x.wait()
-    load_w.wait()
-    load_cos.wait()
-    load_sin.wait()
-    load_owner.wait()
-    load_chosen.wait()
-
-    @pl.when(c == 0)
-    def _():
-        pl.semaphore_wait(barrier, 12)
-
-    @pl.when(c == 1)
-    def _():
-        pl.semaphore_wait(barrier, 22)
-
-    started = []
-    for k, (dy, dl) in enumerate(line[1:]):
-        send(
-            started, x_ref.at[at_y(dy)], xpiece(t, y, c), xy_send.at[k + 1], xy_recv.at[k + 1, c],
-            dev(z, at_y(dy), 1, other(dl) * 4 + x),
-        )
     for k in (2, 3, 0, 1):
         dz, dy = sides[k]
         send(
             started, own_rows, kept(z, y, c), seed_send.at[k], seed_recv.at[k, c], dev(at_z(dz), at_y(dy), 0, t)
         )
-    for k in range(2):
-        send(
-            started, w_ref, wpiece(y, c), w_send.at[k], w_recv.at[k, c], dev(z, at_y(sides[k][1]), 1, t)
-        )
+    for copy in (load_cos, load_sin, load_owner, load_chosen):
+        copy.wait()
 
     @pl.when(c == 0)
     def _():
@@ -321,7 +320,7 @@
             preferred_element_type=jnp.float32,
         )
         zsum[...] = part.reshape(NZ, 2, SEL, KV)
-        for k in range(1, NZ):
+        for k in (4, 3, 5, 2, 6, 1, 7):
             send(
                 pending, zsum.at[at_z(k)], zrecv.at[k], rz_send.at[k], rz_recv.at[k], dev(at_z(k), y, 1, t)
             )
@@ -335,11 +334,10 @@
             keys = keys * trig_c[cc] + pltpu.roll(keys, HD // 2, 1) * trig_s[cc]
             own_fresh[cc, :, :HD] = keys.astype(jnp.bfloat16)
             own_fresh[cc, :, HD:] = fresh[cc, :, HD:].astype(jnp.bfloat16)
-        for k in range(1, NZ):
+        for k in (1, 7, 2, 6, 3, 5, 4):
             send(pending, own_fresh, piece(z, y), fz_send.at[k], fz_recv.at[k], dev(at_z(k), y, 1, t))
         keep_fresh = pltpu.make_async_copy(own_fresh, piece(z, y), local_sem.at[len(loads) + 3])
         keep_fresh.start()
-        keep_fresh.wait()
         def share(d):
             send(pending, column(at_y(d)), column(at_y(d)), fs_send.at[d], fs_recv.at[d], mate)
 
@@ -350,9 +348,10 @@
                 arrived(here, fz_recv.at[rel], fz_send.at[rel])
             for k in range(2):
                 send(
-                    pending, here, here, fy_send.at[rel, k], fy_recv.at[rel, k],
+                    pending, here if rel else own_fresh, here, fy_send.at[rel, k], fy_recv.at[rel, k],
                     dev(z, at_y(sides[k][1]), 1, t),
                 )
+        keep_fresh.wait()
         share(0)
         for rel in near_first:
             zz = at_z(-rel)

time: 58.1 us -> 59.9 us (1.031)
  Pallas kernels: 56 us -> 57.8 us
    pallas_call x1, Pallas kernels: 56 us -> 57.8 us  [local(): pl.pallas_call(kernel, out_shape=jax.ShapeDtypeStruct(queries.shape, jnp....]
where the time goes in v6:
time: 59.9 us; the launch traced here: 59.7 us
  Pallas kernels  57.8 us (96%)
  local copies, waits for them, and re-layouts  1.87 us (3%)
    pallas_call x1, Pallas kernels, local(): pl.pallas_call(kernel, out_shape=jax.ShapeDtypeStruct(queries.shape, jnp....  57.8 us
    unnamed x1, local copies, waits for them, and re-layouts  1.87 us

profile of v6, /device:TPU:1, one launch (start us, length us, event | category | flops | bytes accessed | tf_op | source)
XLA Modules:
  0.0 59.7 jit_solution(5797167963381782540)
XLA Ops:
  0.0 57.8 %shard_map.100 = bf16[8,32,1024]{2,1,0:T(8,128)(2,1)} custom-call(bf16[1,128,256]{2,1,0:T(8,128)(2,1)} %stale_hbm.1, bf16[4,2,16,128]{3,2,1,0:T(8,128)(2,1)} %bitcast.3, bf16[128,2048]{1,0:T(8,128)(2,1)} %w_hbm.1, s32[16,64]{1,0:T(8,128)} %bitcast.4, f32[136,128]{1,0:T(8,128)} %constant.4.clone.cos_hbm, f32[136,128]{1,0:T(8,128)} %constant.5.clone.sin_hbm, ...), custom_call_target="tpu_custom_call" | custom-call | tf_op jit(solution)/shard_map/pallas_call | solution.py:446
  57.8 1.9 %copy.12 = bf16[8,32,1024]{2,1,0:T(8,128)(2,1)} copy(bf16[8,32,1024]{2,1,0:T(8,128)(2,1)} %shard_map.100) | data formatting | bytes 1048576

commit v7 on v4

--- a/solution.py
+++ b/solution.py
@@ -66,17 +66,29 @@
 
     def remote(src, dst, send_sem, recv_sem, device):
         return pltpu.make_async_remote_copy(
-            src_ref=src, dst_ref=dst, send_sem=send_sem, recv_sem=recv_sem,
+            src_ref=src, dst_ref=dst, send_sem=send_sem[0].at[send_sem[1]], recv_sem=recv_sem[0].at[recv_sem[1]],
             device_id=device, device_id_type=MESH,
         )
 
     def arrived(dst, recv_sem, send_sem):
         remote(dst, dst, send_sem, recv_sem, dev(z, y, 1 - c, t)).wait_recv()
 
-    def send(pending, *args):
-        copy = remote(*args)
-        copy.start()
-        pending.append(copy)
+    def send(pending, src, dst, send_sem, recv_sem, device):
+        remote(src, dst, send_sem, recv_sem, device).start()
+        pending.append((tuple(src.shape), jnp.dtype(src.dtype), send_sem, recv_sem))
+
+    def drain(pending):
+        shapes = [
+            pas.at[0, 0, :, pl.ds(0, KEPT)], pas.at[0, 0, 0, pl.ds(0, KEPT)], pas.at[:, 0, :, pl.ds(KEPT, SEL)],
+            pas.at[0, 0, :, pl.ds(KEPT, SEL)], pas.at[0, 0, 0, pl.ds(KEPT, SEL)], x_ref.at[0], w_ref,
+            xbuf.reshape(2, 4, 2, SEL, 8 * HD).at[:, 0], zsum.at[0],
+        ]
+        kinds = {(tuple(ref.shape), jnp.dtype(ref.dtype)): ref for ref in shapes}
+        for shape, kind, send_sem, recv_sem in pending:
+            ref = kinds[shape, kind]
+            remote(ref, ref, send_sem, recv_sem, dev(z, y, 1 - c, t)).wait_send()
+
+    sent = [[], []]
 
     line = [(dy, dl) for dy in range(NY) for dl in range(2)]
     sides = [(0, 1), (0, -1), (1, 0), (-1, 0)]
@@ -182,37 +194,37 @@
     started = []
     for k, (dy, dl) in enumerate(line[1:]):
         send(
-            started, x_ref.at[at_y(dy)], xpiece(t, y, c), xy_send.at[k + 1], xy_recv.at[k + 1, c],
+            started, x_ref.at[at_y(dy)], xpiece(t, y, c), (xy_send, (k + 1,)), (xy_recv, (k + 1, c,)),
             dev(z, at_y(dy), 1, other(dl) * 4 + x),
         )
     for k in (2, 3, 0, 1):
         dz, dy = sides[k]
         send(
-            started, own_rows, kept(z, y, c), seed_send.at[k], seed_recv.at[k, c], dev(at_z(dz), at_y(dy), 0, t)
+            started, own_rows, kept(z, y, c), (seed_send, (k,)), (seed_recv, (k, c,)), dev(at_z(dz), at_y(dy), 0, t)
         )
     for k in range(2):
         send(
-            started, w_ref, wpiece(y, c), w_send.at[k], w_recv.at[k, c], dev(z, at_y(sides[k][1]), 1, t)
+            started, w_ref, wpiece(y, c), (w_send, (k,)), (w_recv, (k, c,)), dev(z, at_y(sides[k][1]), 1, t)
         )
 
     @pl.when(c == 0)
     def _():
-        pending = []
+        pending = sent[0]
         mate = dev(z, y, 1, t)
-        send(pending, x_ref.at[y], xpiece(t, y, 0), xy_send.at[0], xy_recv.at[0, 0], mate)
-        send(pending, w_ref, wpiece(y, 0), w_send.at[2], w_recv.at[2, 0], mate)
+        send(pending, x_ref.at[y], xpiece(t, y, 0), (xy_send, (0,)), (xy_recv, (0, 0,)), mate)
+        send(pending, w_ref, wpiece(y, 0), (w_send, (2,)), (w_recv, (2, 0,)), mate)
         own_copy = pltpu.make_async_copy(own_rows, kept(z, y, 0), local_sem.at[len(loads)])
         own_copy.start()
 
         def ring(zz, yy, s, d, way):
             step = 1 if way == 0 else -1
             send(
-                pending, chunk(zz, yy), chunk(zz, yy), sz_send.at[way, s, d], sz_recv.at[way, s, d],
+                pending, chunk(zz, yy), chunk(zz, yy), (sz_send, (way, s, d,)), (sz_recv, (way, s, d,)),
                 dev(at_z(step), y, 0, t),
             )
 
         def share(zz, yy, rel, d):
-            send(pending, chunk(zz, yy), chunk(zz, yy), ss_send.at[rel, d], ss_recv.at[rel, d], mate)
+            send(pending, chunk(zz, yy), chunk(zz, yy), (ss_send, (rel, d,)), (ss_recv, (rel, d,)), mate)
 
         def inject(d):
             for way in range(2):
@@ -230,15 +242,15 @@
                 zz, yy = at_z(rel), at_y(d)
                 if s == 1 and d == 0:
                     for cc in range(2):
-                        arrived(kept(zz, yy, cc), seed_recv.at[2 + way, cc], seed_send.at[2 + way])
+                        arrived(kept(zz, yy, cc), (seed_recv, (2 + way, cc,)), (seed_send, (2 + way,)))
                 else:
-                    arrived(chunk(zz, yy), sz_recv.at[way, s, d], sz_send.at[way, s, d])
-                if s < (2 if d == 2 else 3) or (s == 3 and way == last_way(d)):
+                    arrived(chunk(zz, yy), (sz_recv, (way, s, d,)), (sz_send, (way, s, d,)))
+                if (s < 3 and d != 2) or (s == 3 and way == last_way(d)):
                     ring(zz, yy, s + 1, d, way)
-                if s >= 3 and d:
+                if s >= 2 and d:
                     k = 0 if d == 3 else 1
                     send(
-                        pending, kept(zz, yy, k), kept(zz, yy, k), yf_send.at[rel, k], yf_recv.at[rel, k],
+                        pending, kept(zz, yy, k), kept(zz, yy, k), (yf_send, (rel, k,)), (yf_recv, (rel, k,)),
                         dev(z, at_y(sides[k][1]), 0, t),
                     )
                 share(zz, yy, rel, d)
@@ -247,9 +259,9 @@
         for k in range(2):
             yy = at_y(-sides[k][1])
             for cc in range(2):
-                arrived(kept(z, yy, cc), seed_recv.at[k, cc], seed_send.at[k])
+                arrived(kept(z, yy, cc), (seed_recv, (k, cc,)), (seed_send, (k,)))
             send(
-                pending, kept(z, yy, k), kept(z, yy, k), yr_send.at[k], yr_recv.at[k],
+                pending, kept(z, yy, k), kept(z, yy, k), (yr_send, (k,)), (yr_recv, (k,)),
                 dev(z, at_y(sides[k][1]), 0, t),
             )
             inject(3 if k == 0 else 1)
@@ -257,27 +269,25 @@
         hop(1, 3)
         hop(1, 1)
         for k in range(2):
-            arrived(kept(z, at_y(2), k), yr_recv.at[k], yr_send.at[k])
+            arrived(kept(z, at_y(2), k), (yr_recv, (k,)), (yr_send, (k,)))
         inject(2)
         own_copy.wait()
-        arrived(kept(z, y, 1), ss_recv.at[0, 0], ss_send.at[0, 0])
-        send(pending, kept(z, y, 0), kept(z, y, 0), ss_send.at[0, 0], ss_recv.at[0, 0], mate)
+        arrived(kept(z, y, 1), (ss_recv, (0, 0,)), (ss_send, (0, 0,)))
+        send(pending, kept(z, y, 0), kept(z, y, 0), (ss_send, (0, 0,)), (ss_recv, (0, 0,)), mate)
         for s, d in (
-            (3, 0), (2, 3), (2, 1), (1, 2), (4, 0), (3, 3), (3, 1), (2, 2), (4, 3), (4, 1),
+            (3, 0), (2, 3), (2, 1), (1, 2), (4, 0), (3, 3), (3, 1), (4, 3), (4, 1),
         ):
             hop(s, d)
-        for rel in (5, 3, 4):
+        for rel in (6, 2, 5, 3, 4):
             for k in range(2):
-                arrived(kept(at_z(rel), at_y(2), k), yf_recv.at[rel, k], yf_send.at[rel, k])
+                arrived(kept(at_z(rel), at_y(2), k), (yf_recv, (rel, k,)), (yf_send, (rel, k,)))
             share(at_z(rel), at_y(2), rel, 2)
         for d in range(NY):
-            arrived(column(at_y(d)), fs_recv.at[d], fs_send.at[d])
-        for copy in pending:
-            copy.wait_send()
+            arrived(column(at_y(d)), (fs_recv, (d,)), (fs_send, (d,)))
 
     @pl.when(c == 1)
     def _():
-        pending = []
+        pending = sent[1]
         mate = dev(z, y, 0, t)
         own_x = pltpu.make_async_copy(x_ref.at[y], xpiece(t, y, 1), local_sem.at[len(loads)])
         own_w = pltpu.make_async_copy(w_ref, wpiece(y, 1), local_sem.at[len(loads) + 1])
@@ -285,23 +295,23 @@
         own_x.start()
         own_w.start()
         own_copy.start()
-        send(pending, own_rows, kept(z, y, 1), ss_send.at[0, 0], ss_recv.at[0, 0], mate)
+        send(pending, own_rows, kept(z, y, 1), (ss_send, (0, 0,)), (ss_recv, (0, 0,)), mate)
         own_x.wait()
-        arrived(xpiece(t, y, 0), xy_recv.at[0, 0], xy_send.at[0])
+        arrived(xpiece(t, y, 0), (xy_recv, (0, 0,)), (xy_send, (0,)))
         for k, (dy, dl) in enumerate(line[1:]):
             for cc in range(2):
-                arrived(xpiece(other(dl) * 4 + x, at_y(-dy), cc), xy_recv.at[k + 1, cc], xy_send.at[k + 1])
+                arrived(xpiece(other(dl) * 4 + x, at_y(-dy), cc), (xy_recv, (k + 1, cc,)), (xy_send, (k + 1,)))
         xall = xbuf.reshape(2, 4, 2, SEL, 8 * HD)
         for k in range(1, NX):
             send(
-                pending, xall.at[:, x], xall.at[:, x], xx_send.at[k], xx_recv.at[k], (r, ylo * 4 + at_x(k))
+                pending, xall.at[:, x], xall.at[:, x], (xx_send, (k,)), (xx_recv, (k,)), (r, ylo * 4 + at_x(k))
             )
         for k in range(2):
             yy = at_y(-sides[k][1])
             for cc in range(2):
-                arrived(wpiece(yy, cc), w_recv.at[k, cc], w_send.at[k])
+                arrived(wpiece(yy, cc), (w_recv, (k, cc,)), (w_send, (k,)))
             send(
-                pending, wpiece(yy, k), wpiece(yy, k), wr_send.at[k], wr_recv.at[k],
+                pending, wpiece(yy, k), wpiece(yy, k), (wr_send, (k,)), (wr_recv, (k,)),
                 dev(z, at_y(sides[k][1]), 1, t),
             )
         for cc in range(2):
@@ -310,11 +320,11 @@
                 trig_c[cc, pl.ds(k, 1), :] = cos_ref[pl.ds(position, 1), :]
                 trig_s[cc, pl.ds(k, 1), :] = sin_ref[pl.ds(position, 1), :]
         own_w.wait()
-        arrived(wpiece(y, 0), w_recv.at[2, 0], w_send.at[2])
+        arrived(wpiece(y, 0), (w_recv, (2, 0,)), (w_send, (2,)))
         for k in range(1, NX):
-            arrived(xall.at[:, at_x(-k)], xx_recv.at[k], xx_send.at[k])
+            arrived(xall.at[:, at_x(-k)], (xx_recv, (k,)), (xx_send, (k,)))
         for k in range(2):
-            arrived(wpiece(at_y(2), k), wr_recv.at[k], wr_send.at[k])
+            arrived(wpiece(at_y(2), k), (wr_recv, (k,)), (wr_send, (k,)))
         part = jnp.dot(
             xbuf[...].reshape(NZ * 2 * SEL, 8 * HD),
             wbuf[...].reshape(8 * HD, KV),
@@ -323,11 +333,11 @@
         zsum[...] = part.reshape(NZ, 2, SEL, KV)
         for k in range(1, NZ):
             send(
-                pending, zsum.at[at_z(k)], zrecv.at[k], rz_send.at[k], rz_recv.at[k], dev(at_z(k), y, 1, t)
+                pending, zsum.at[at_z(k)], zrecv.at[k], (rz_send, (k,)), (rz_recv, (k,)), dev(at_z(k), y, 1, t)
             )
         total = zsum[z]
         for k in range(1, NZ):
-            arrived(zrecv.at[k], rz_recv.at[k], rz_send.at[k])
+            arrived(zrecv.at[k], (rz_recv, (k,)), (rz_send, (k,)))
             total = total + zrecv[k]
         fresh = total.astype(jnp.bfloat16).astype(jnp.float32)
         for cc in range(2):
@@ -336,21 +346,21 @@
             own_fresh[cc, :, :HD] = keys.astype(jnp.bfloat16)
             own_fresh[cc, :, HD:] = fresh[cc, :, HD:].astype(jnp.bfloat16)
         for k in range(1, NZ):
-            send(pending, own_fresh, piece(z, y), fz_send.at[k], fz_recv.at[k], dev(at_z(k), y, 1, t))
+            send(pending, own_fresh, piece(z, y), (fz_send, (k,)), (fz_recv, (k,)), dev(at_z(k), y, 1, t))
         keep_fresh = pltpu.make_async_copy(own_fresh, piece(z, y), local_sem.at[len(loads) + 3])
         keep_fresh.start()
         keep_fresh.wait()
         def share(d):
-            send(pending, column(at_y(d)), column(at_y(d)), fs_send.at[d], fs_recv.at[d], mate)
+            send(pending, column(at_y(d)), column(at_y(d)), (fs_send, (d,)), (fs_recv, (d,)), mate)
 
         near_first = (0, 1, 7, 2, 6, 3, 5, 4)
         for rel in near_first:
             here = piece(at_z(-rel), y)
             if rel:
-                arrived(here, fz_recv.at[rel], fz_send.at[rel])
+                arrived(here, (fz_recv, (rel,)), (fz_send, (rel,)))
             for k in range(2):
                 send(
-                    pending, here, here, fy_send.at[rel, k], fy_recv.at[rel, k],
+                    pending, here, here, (fy_send, (rel, k,)), (fy_recv, (rel, k,)),
                     dev(z, at_y(sides[k][1]), 1, t),
                 )
         share(0)
@@ -358,28 +368,23 @@
             zz = at_z(-rel)
             for k in range(2):
                 yy = at_y(-sides[k][1])
-                arrived(piece(zz, yy), fy_recv.at[rel, k], fy_send.at[rel, k])
+                arrived(piece(zz, yy), (fy_recv, (rel, k,)), (fy_send, (rel, k,)))
                 send(
-                    pending, half_piece(zz, yy, k), half_piece(zz, yy, k), fr_send.at[rel, k], fr_recv.at[rel, k],
+                    pending, half_piece(zz, yy, k), half_piece(zz, yy, k), (fr_send, (rel, k,)), (fr_recv, (rel, k,)),
                     dev(z, at_y(sides[k][1]), 1, t),
                 )
         share(3)
         share(1)
         for rel in near_first:
             for k in range(2):
-                arrived(half_piece(at_z(-rel), at_y(2), k), fr_recv.at[rel, k], fr_send.at[rel, k])
+                arrived(half_piece(at_z(-rel), at_y(2), k), (fr_recv, (rel, k,)), (fr_send, (rel, k,)))
         share(2)
         own_copy.wait()
-        arrived(kept(z, y, 0), ss_recv.at[0, 0], ss_send.at[0, 0])
+        arrived(kept(z, y, 0), (ss_recv, (0, 0,)), (ss_send, (0, 0,)))
         for rel in range(NZ):
             for d in range(NY):
                 if rel or d:
-                    arrived(chunk(at_z(rel), at_y(d)), ss_recv.at[rel, d], ss_send.at[rel, d])
-        for copy in pending:
-            copy.wait_send()
-
-    for copy in started:
-        copy.wait_send()
+                    arrived(chunk(at_z(rel), at_y(d)), (ss_recv, (rel, d,)), (ss_send, (rel, d,)))
 
     kbufs, vbufs, sbufs, pbufs = (kbuf0, kbuf1), (vbuf0, vbuf1), (sbuf0, sbuf1), (pbuf0, pbuf1)
     steps = q_ref.shape[0] // PAIR
@@ -437,6 +442,12 @@
     lax.fori_loop(0, steps, pair, 0)
     for step in range(steps):
         result_copy(step).wait()
+    drain(started)
+    for core in range(2):
+
+        @pl.when(c == core)
+        def _(core=core):
+            drain(sent[core])
 
 
 def local(stale, fresh_input, kv_weight, sel_index, owner, retrieval, queries, question_kv):

time: 58.1 us -> 58.5 us (level)
  no operation moved by 1% of the time
where the time goes in v7:
time: 58.5 us; the launch traced here: 58.4 us
  Pallas kernels  56.5 us (97%)
  local copies, waits for them, and re-layouts  1.87 us (3%)
    pallas_call x1, Pallas kernels, local(): pl.pallas_call(kernel, out_shape=jax.ShapeDtypeStruct(queries.shape, jnp....  56.5 us
    unnamed x1, local copies, waits for them, and re-layouts  1.87 us

profile of v7, /device:TPU:1, one launch (start us, length us, event | category | flops | bytes accessed | tf_op | source)
XLA Modules:
  0.0 58.4 jit_solution(4615638614050410784)
XLA Ops:
  0.0 56.5 %shard_map.100 = bf16[8,32,1024]{2,1,0:T(8,128)(2,1)} custom-call(bf16[1,128,256]{2,1,0:T(8,128)(2,1)} %stale_hbm.1, bf16[4,2,16,128]{3,2,1,0:T(8,128)(2,1)} %bitcast.3, bf16[128,2048]{1,0:T(8,128)(2,1)} %w_hbm.1, s32[16,64]{1,0:T(8,128)} %bitcast.4, f32[136,128]{1,0:T(8,128)} %constant.4.clone.cos_hbm, f32[136,128]{1,0:T(8,128)} %constant.5.clone.sin_hbm, ...), custom_call_target="tpu_custom_call" | custom-call | tf_op jit(solution)/shard_map/pallas_call | solution.py:458
  56.5 1.9 %copy.12 = bf16[8,32,1024]{2,1,0:T(8,128)(2,1)} copy(bf16[8,32,1024]{2,1,0:T(8,128)(2,1)} %shard_map.100) | data formatting | bytes 1048576

commit v8 on v7

--- a/solution.py
+++ b/solution.py
@@ -160,6 +160,22 @@
         later.append(pltpu.make_async_copy(source, target, q_sem.at[k]))
         later[-1].start()
 
+    load_x.wait()
+
+    @pl.when(c == 0)
+    def _():
+        pl.semaphore_wait(barrier, 12)
+
+    @pl.when(c == 1)
+    def _():
+        pl.semaphore_wait(barrier, 22)
+
+    started = []
+    for k, (dy, dl) in enumerate(line[1:]):
+        send(
+            started, x_ref.at[at_y(dy)], xpiece(t, y, c), (xy_send, (k + 1,)), (xy_recv, (k + 1, c,)),
+            dev(z, at_y(dy), 1, other(dl) * 4 + x),
+        )
     load_sel.wait()
     lane = lax.broadcasted_iota(jnp.int32, (8, PLEN), 1)
     hit = lane == sel_ref[0, r]
@@ -176,36 +192,19 @@
     picked = jnp.where(order == rank[0:1], keep[0:1], jnp.float32(0.0)).astype(jnp.bfloat16)
     load_stale.wait()
     own_rows[...] = jnp.dot(picked, stale_ref[...], preferred_element_type=jnp.float32).astype(jnp.bfloat16)
-    load_x.wait()
-    load_w.wait()
-    load_cos.wait()
-    load_sin.wait()
-    load_owner.wait()
-    load_chosen.wait()
-
-    @pl.when(c == 0)
-    def _():
-        pl.semaphore_wait(barrier, 12)
-
-    @pl.when(c == 1)
-    def _():
-        pl.semaphore_wait(barrier, 22)
-
-    started = []
-    for k, (dy, dl) in enumerate(line[1:]):
-        send(
-            started, x_ref.at[at_y(dy)], xpiece(t, y, c), (xy_send, (k + 1,)), (xy_recv, (k + 1, c,)),
-            dev(z, at_y(dy), 1, other(dl) * 4 + x),
-        )
     for k in (2, 3, 0, 1):
         dz, dy = sides[k]
         send(
             started, own_rows, kept(z, y, c), (seed_send, (k,)), (seed_recv, (k, c,)), dev(at_z(dz), at_y(dy), 0, t)
         )
+    load_w.wait()
     for k in range(2):
         send(
             started, w_ref, wpiece(y, c), (w_send, (k,)), (w_recv, (k, c,)), dev(z, at_y(sides[k][1]), 1, t)
         )
+
+    for copy in (load_cos, load_sin, load_owner, load_chosen):
+        copy.wait()
 
     @pl.when(c == 0)
     def _():
@@ -331,7 +330,7 @@
             preferred_element_type=jnp.float32,
         )
         zsum[...] = part.reshape(NZ, 2, SEL, KV)
-        for k in range(1, NZ):
+        for k in (4, 3, 5, 2, 6, 1, 7):
             send(
                 pending, zsum.at[at_z(k)], zrecv.at[k], (rz_send, (k,)), (rz_recv, (k,)), dev(at_z(k), y, 1, t)
             )
@@ -345,11 +344,10 @@
             keys = keys * trig_c[cc] + pltpu.roll(keys, HD // 2, 1) * trig_s[cc]
             own_fresh[cc, :, :HD] = keys.astype(jnp.bfloat16)
             own_fresh[cc, :, HD:] = fresh[cc, :, HD:].astype(jnp.bfloat16)
-        for k in range(1, NZ):
+        for k in (1, 7, 2, 6, 3, 5, 4):
             send(pending, own_fresh, piece(z, y), (fz_send, (k,)), (fz_recv, (k,)), dev(at_z(k), y, 1, t))
         keep_fresh = pltpu.make_async_copy(own_fresh, piece(z, y), local_sem.at[len(loads) + 3])
         keep_fresh.start()
-        keep_fresh.wait()
         def share(d):
             send(pending, column(at_y(d)), column(at_y(d)), (fs_send, (d,)), (fs_recv, (d,)), mate)
 
@@ -360,9 +358,10 @@
                 arrived(here, (fz_recv, (rel,)), (fz_send, (rel,)))
             for k in range(2):
                 send(
-                    pending, here, here, (fy_send, (rel, k,)), (fy_recv, (rel, k,)),
+                    pending, here if rel else own_fresh, here, (fy_send, (rel, k,)), (fy_recv, (rel, k,)),
                     dev(z, at_y(sides[k][1]), 1, t),
                 )
+        keep_fresh.wait()
         share(0)
         for rel in near_first:
             zz = at_z(-rel)

time: 58.5 us -> 58.9 us (level)
  no operation moved by 1% of the time
where the time goes in v8:
time: 58.9 us; the launch traced here: 58.8 us
  Pallas kernels  56.9 us (97%)
  local copies, waits for them, and re-layouts  1.87 us (3%)
    pallas_call x1, Pallas kernels, local(): pl.pallas_call(kernel, out_shape=jax.ShapeDtypeStruct(queries.shape, jnp....  56.9 us
    unnamed x1, local copies, waits for them, and re-layouts  1.87 us

profile of v8, /device:TPU:1, one launch (start us, length us, event | category | flops | bytes accessed | tf_op | source)
XLA Modules:
  0.0 58.8 jit_solution(8772077516235266705)
XLA Ops:
  0.0 56.9 %shard_map.100 = bf16[8,32,1024]{2,1,0:T(8,128)(2,1)} custom-call(bf16[1,128,256]{2,1,0:T(8,128)(2,1)} %stale_hbm.1, bf16[4,2,16,128]{3,2,1,0:T(8,128)(2,1)} %bitcast.3, bf16[128,2048]{1,0:T(8,128)(2,1)} %w_hbm.1, s32[16,64]{1,0:T(8,128)} %bitcast.4, f32[136,128]{1,0:T(8,128)} %constant.4.clone.cos_hbm, f32[136,128]{1,0:T(8,128)} %constant.5.clone.sin_hbm, ...), custom_call_target="tpu_custom_call" | custom-call | tf_op jit(solution)/shard_map/pallas_call | solution.py:457
  56.9 1.9 %copy.12 = bf16[8,32,1024]{2,1,0:T(8,128)(2,1)} copy(bf16[8,32,1024]{2,1,0:T(8,128)(2,1)} %shard_map.100) | data formatting | bytes 1048576

commit v9 on v8

--- a/solution.py
+++ b/solution.py
@@ -432,7 +432,7 @@
                 raw = jnp.concatenate([sbuf[rows, :LAST], sbuf[rows, LAST:] + tail], 1)
                 expo = jnp.exp2((raw - jnp.max(raw, 1, keepdims=True)) * SCALE)
                 pbuf[rows, :] = (expo * (1.0 / jnp.sum(expo, 1, keepdims=True))).astype(jnp.bfloat16)
-            result = jnp.dot(pbuf[...], vbufs[i][...], preferred_element_type=jnp.float32).astype(jnp.bfloat16)
+            result = jnp.dot(pbuf[...], vbufs[i][...], preferred_element_type=jnp.float32)
             for h in range(GROUP):
                 out_ref[step * PAIR + i, :, h * HD : (h + 1) * HD] = result[h * QLEN : (h + 1) * QLEN]
         result_copy(step).start()
@@ -456,7 +456,7 @@
     rows = GROUP * QLEN
     return pl.pallas_call(
         kernel,
-        out_shape=jax.ShapeDtypeStruct(queries.shape, jnp.bfloat16),
+        out_shape=jax.ShapeDtypeStruct(queries.shape, jnp.float32),
         in_specs=[any_spec] * 10,
         out_specs=any_spec,
         scratch_shapes=[
@@ -471,7 +471,7 @@
             pltpu.VMEM((rows, KEYS), jnp.bfloat16),
             pltpu.VMEM(queries.shape, jnp.bfloat16),
             pltpu.VMEM(question_kv.shape, jnp.bfloat16),
-            pltpu.VMEM(queries.shape, jnp.bfloat16),
+            pltpu.VMEM(queries.shape, jnp.float32),
             pltpu.SMEM((64,), jnp.int32),
             pltpu.SMEM((SLOTS, 8), jnp.int32),
             pltpu.VMEM((PLEN, KV), jnp.bfloat16),
@@ -519,7 +519,7 @@
         retrieval.T,
         queries,
         question_kv,
-    )
+    ).astype(jnp.bfloat16)
 
 
 def solution(mesh):

time: 58.9 us -> 59.2 us (level)
  other arithmetic: 0 us -> 2.1 us
  local copies, waits for them, and re-layouts: 1.87 us -> 0 us
    convert_element_type x0 -> x1, other arithmetic: none -> 2.1 us  [local(): return pl.pallas_call(kernel, out_shape=jax.ShapeDtypeStruct(queries.shap...]
    unnamed x1 -> x0, local copies, waits for them, and re-layouts: 1.87 us -> none
where the time goes in v9:
time: 59.2 us; the launch traced here: 59 us
  Pallas kernels  56.9 us (96%)
  other arithmetic  2.1 us (4%)
    pallas_call x1, Pallas kernels, local(): pl.pallas_call(kernel, out_shape=jax.ShapeDtypeStruct(queries.shape, jnp....  56.9 us
    convert_element_type x1, other arithmetic, local(): return pl.pallas_call(kernel, out_shape=jax.ShapeDtypeStruct(queries.shap...  2.1 us

profile of v9, /device:TPU:1, one launch (start us, length us, event | category | flops | bytes accessed | tf_op | source)
XLA Modules:
  0.0 59.0 jit_solution(2102651215568391411)
XLA Ops:
  0.0 56.9 %shard_map.100 = f32[8,32,1024]{2,1,0:T(8,128)} custom-call(bf16[1,128,256]{2,1,0:T(8,128)(2,1)} %stale_hbm.1, bf16[4,2,16,128]{3,2,1,0:T(8,128)(2,1)} %bitcast.3, bf16[128,2048]{1,0:T(8,128)(2,1)} %w_hbm.1, s32[16,64]{1,0:T(8,128)} %bitcast.4, f32[136,128]{1,0:T(8,128)} %constant.4.clone.cos_hbm, f32[136,128]{1,0:T(8,128)} %constant.5.clone.sin_hbm, ...), custom_call_target="tpu_custom_call" | custom-call | tf_op jit(solution)/shard_map/pallas_call | solution.py:457
  56.9 2.1 %convert_element_type.3 = bf16[8,32,1024]{2,1,0:T(8,128)(2,1)} convert(f32[8,32,1024]{2,1,0:T(8,128)} %shard_map.100) | non-fusion elementwise | flops 262144 | bytes 1572864 | tf_op jit(solution)/shard_map/convert_element_type | solution.py:522

commit v10 on v8

--- a/solution.py
+++ b/solution.py
@@ -244,9 +244,9 @@
                         arrived(kept(zz, yy, cc), (seed_recv, (2 + way, cc,)), (seed_send, (2 + way,)))
                 else:
                     arrived(chunk(zz, yy), (sz_recv, (way, s, d,)), (sz_send, (way, s, d,)))
-                if (s < 3 and d != 2) or (s == 3 and way == last_way(d)):
+                if s < (2 if d == 2 else 3) or (s == 3 and way == last_way(d)):
                     ring(zz, yy, s + 1, d, way)
-                if s >= 2 and d:
+                if s >= 3 and d:
                     k = 0 if d == 3 else 1
                     send(
                         pending, kept(zz, yy, k), kept(zz, yy, k), (yf_send, (rel, k,)), (yf_recv, (rel, k,)),
@@ -274,10 +274,10 @@
         arrived(kept(z, y, 1), (ss_recv, (0, 0,)), (ss_send, (0, 0,)))
         send(pending, kept(z, y, 0), kept(z, y, 0), (ss_send, (0, 0,)), (ss_recv, (0, 0,)), mate)
         for s, d in (
-            (3, 0), (2, 3), (2, 1), (1, 2), (4, 0), (3, 3), (3, 1), (4, 3), (4, 1),
+            (3, 0), (2, 3), (2, 1), (1, 2), (4, 0), (3, 3), (3, 1), (2, 2), (4, 3), (4, 1),
         ):
             hop(s, d)
-        for rel in (6, 2, 5, 3, 4):
+        for rel in (5, 3, 4):
             for k in range(2):
                 arrived(kept(at_z(rel), at_y(2), k), (yf_recv, (rel, k,)), (yf_send, (rel, k,)))
             share(at_z(rel), at_y(2), rel, 2)

time: 58.9 us -> 58.5 us (level)
  no operation moved by 1% of the time
where the time goes in v10:
time: 58.5 us; the launch traced here: 58.3 us
  Pallas kernels  56.4 us (96%)
  local copies, waits for them, and re-layouts  1.87 us (3%)
    pallas_call x1, Pallas kernels, local(): pl.pallas_call(kernel, out_shape=jax.ShapeDtypeStruct(queries.shape, jnp....  56.4 us
    unnamed x1, local copies, waits for them, and re-layouts  1.87 us

profile of v10, /device:TPU:1, one launch (start us, length us, event | category | flops | bytes accessed | tf_op | source)
XLA Modules:
  0.0 58.3 jit_solution(9820224423910695520)
XLA Ops:
  0.0 56.4 %shard_map.100 = bf16[8,32,1024]{2,1,0:T(8,128)(2,1)} custom-call(bf16[1,128,256]{2,1,0:T(8,128)(2,1)} %stale_hbm.1, bf16[4,2,16,128]{3,2,1,0:T(8,128)(2,1)} %bitcast.3, bf16[128,2048]{1,0:T(8,128)(2,1)} %w_hbm.1, s32[16,64]{1,0:T(8,128)} %bitcast.4, f32[136,128]{1,0:T(8,128)} %constant.4.clone.cos_hbm, f32[136,128]{1,0:T(8,128)} %constant.5.clone.sin_hbm, ...), custom_call_target="tpu_custom_call" | custom-call | tf_op jit(solution)/shard_map/pallas_call | solution.py:457
  56.4 1.9 %copy.12 = bf16[8,32,1024]{2,1,0:T(8,128)(2,1)} copy(bf16[8,32,1024]{2,1,0:T(8,128)(2,1)} %shard_map.100) | data formatting | bytes 1048576
